TPU v7x, 256 devices: a whole 4x4x8 slice. The times are simulated.
256 devices in a mesh: rep: 4 (over x), ep: 64 (over y, z, core).
Axes of the slice: x: 4, y: 4, z: 8, core: 2. Of those that a mesh axis runs over, the one named last changes fastest.
Arguments:
- tokens: bfloat16 [32768, 4096], P(('rep', 'ep')), may hold values from -6 to 6
- cotangent: bfloat16 [32768, 4096], P(('rep', 'ep')), may hold values from -6 to 6
- expert_ids: int32 [32768, 1], P(('rep', 'ep')), may hold values from 0 to 63; in each aligned block of 128 rows (0 to 127, 128 to 255, ...) at most 4 rows name the same one
- gates: bfloat16 [32768, 1], P(('rep', 'ep')), may hold values from 0.19921875 to 1.5
- gate_weight: bfloat16 [64, 4096, 768], P('ep', None, 'rep'), may hold values from -0.09375 to 0.09375
- up_weight: bfloat16 [64, 4096, 768], P('ep', None, 'rep'), may hold values from -0.09375 to 0.09375
- down_weight: bfloat16 [64, 768, 4096], P('ep', 'rep'), may hold values from -0.21875 to 0.21875
Outputs:
- token_grad: bfloat16 [32768, 4096], P(('rep', 'ep'))
- gates_grad: bfloat16 [32768, 1], P(('rep', 'ep'))
- gate_weight_grad: bfloat16 [64, 4096, 768], P('ep', None, 'rep')
- up_weight_grad: bfloat16 [64, 4096, 768], P('ep', None, 'rep')
- down_weight_grad: bfloat16 [64, 768, 4096], P('ep', 'rep')
Inputs may be any that keep to these rules, and one draw needn't show every extreme that they name: `expert_ids`: each token names exactly 1 expert. Within the rows of one device (aligned blocks of 128 tokens) no expert is named by more than 4 rows, a bound that some block reaches.
All inputs are finite; a program needn't handle non-finite values.
Results may differ from a plain program's by a relative error of at most 0.02.
Values may be sent and summed in bfloat16 or wider, within the bound.
A program may use at most 192 MiB of HBM per device.

v0:
```python
import jax
import jax.numpy as jnp
from jax import lax
from jax.sharding import PartitionSpec as P


def shards(tokens, cotangent, expert_ids, gates, gate_weight, up_weight, down_weight):
    peer_count = lax.axis_size("ep")
    replica_count = lax.axis_size("rep")
    tok_rows, width = tokens.shape
    picks = expert_ids.shape[1]
    local_experts = gate_weight.shape[0]
    expert_total = local_experts * peer_count
    row_total = tok_rows * picks
    capacity = 2 * row_total // expert_total
    slot_rows = local_experts * capacity
    groups = replica_count * peer_count
    flat = expert_ids.reshape(-1)
    onehot = (flat[:, None] == jnp.arange(expert_total, dtype=jnp.int32)[None, :]).astype(jnp.int32)
    ranks = jnp.sum((jnp.cumsum(onehot, axis=0) - 1) * onehot, axis=1)
    slots = flat * capacity + ranks
    input_rows = jnp.repeat(tokens, picks, axis=0)
    cotan_rows = jnp.repeat(cotangent, picks, axis=0)
    input_buf = jnp.zeros((expert_total * capacity, width), jnp.bfloat16).at[slots].set(input_rows)
    cotan_buf = jnp.zeros((expert_total * capacity, width), jnp.bfloat16).at[slots].set(cotan_rows)
    weight_buf = (
        jnp.zeros((expert_total * capacity,), jnp.bfloat16).at[slots].set(gates.reshape(-1))
    )
    input_buf = input_buf.reshape(peer_count, slot_rows, width)
    cotan_buf = cotan_buf.reshape(peer_count, slot_rows, width)
    weight_buf = weight_buf.reshape(peer_count, slot_rows)
    input_recv, cotan_recv, weight_recv = (
        lax.all_to_all(input_buf, "ep", split_axis=0, concat_axis=0, tiled=True),
        lax.all_to_all(cotan_buf, "ep", split_axis=0, concat_axis=0, tiled=True),
        lax.all_to_all(weight_buf, "ep", split_axis=0, concat_axis=0, tiled=True),
    )
    input_all, cotan_all, weight_all = (
        lax.all_gather(input_recv, "rep", axis=0, tiled=True),
        lax.all_gather(cotan_recv, "rep", axis=0, tiled=True),
        lax.all_gather(weight_recv, "rep", axis=0, tiled=True),
    )
    inputs = input_all.reshape(groups, local_experts, capacity, width)
    cotan = cotan_all.reshape(groups, local_experts, capacity, width)
    weight = weight_all.reshape(groups, local_experts, capacity).astype(jnp.float32)[..., None]
    gate_pre = jnp.einsum("secd,edh->sech", inputs, gate_weight, preferred_element_type=jnp.float32)
    up_pre = jnp.einsum("secd,edh->sech", inputs, up_weight, preferred_element_type=jnp.float32)
    logistic = jax.nn.sigmoid(gate_pre)
    activated = gate_pre * logistic
    hidden = (activated * up_pre).astype(jnp.bfloat16)
    hidden_grad = jnp.einsum(
        "secd,ehd->sech", cotan, down_weight, preferred_element_type=jnp.float32
    )
    gate_part = jnp.sum(hidden.astype(jnp.float32) * hidden_grad, axis=3)
    weighted = hidden_grad * weight
    pre_grad = (weighted * up_pre * logistic * (1.0 + gate_pre * (1.0 - logistic))).astype(
        jnp.bfloat16
    )
    up_grad = (weighted * activated).astype(jnp.bfloat16)
    scaled_cot = (cotan * weight).astype(jnp.bfloat16)
    down_grad = jnp.einsum(
        "sech,secd->ehd", hidden, scaled_cot, preferred_element_type=jnp.float32
    ).astype(jnp.bfloat16)
    gate_grad = jnp.einsum(
        "secd,sech->edh", inputs, pre_grad, preferred_element_type=jnp.float32
    ).astype(jnp.bfloat16)
    upper_grad = jnp.einsum(
        "secd,sech->edh", inputs, up_grad, preferred_element_type=jnp.float32
    ).astype(jnp.bfloat16)
    part = jnp.einsum("sech,edh->secd", pre_grad, gate_weight, preferred_element_type=jnp.float32)
    part = part + jnp.einsum(
        "sech,edh->secd", up_grad, up_weight, preferred_element_type=jnp.float32
    )
    part = part.astype(jnp.bfloat16).reshape(groups, slot_rows, width)
    part_gates = gate_part.astype(jnp.bfloat16).reshape(groups, slot_rows)
    summed_rows, summed_gates = (
        lax.psum_scatter(part, "rep", scatter_dimension=0, tiled=True).astype(jnp.float32),
        lax.psum_scatter(part_gates, "rep", scatter_dimension=0, tiled=True).astype(jnp.float32),
    )
    row_grad = summed_rows.astype(jnp.bfloat16)
    gate_total = summed_gates.astype(jnp.bfloat16)
    rows_back, gates_back = (
        lax.all_to_all(row_grad, "ep", split_axis=0, concat_axis=0, tiled=True),
        lax.all_to_all(gate_total, "ep", split_axis=0, concat_axis=0, tiled=True),
    )
    per_row = rows_back.reshape(expert_total * capacity, width)[slots]
    token_grad = jnp.sum(
        per_row.astype(jnp.float32).reshape(tok_rows, picks, width), axis=1
    ).astype(jnp.bfloat16)
    gates_grad = gates_back.reshape(-1)[slots].reshape(tok_rows, picks)
    return (token_grad, gates_grad, gate_grad, upper_grad, down_grad)


def solution(mesh):
    in_specs = (
        P(("rep", "ep"), None),
        P(("rep", "ep"), None),
        P(("rep", "ep"), None),
        P(("rep", "ep"), None),
        P("ep", None, "rep"),
        P("ep", None, "rep"),
        P("ep", "rep", None),
    )
    out_specs = (
        P(("rep", "ep"), None),
        P(("rep", "ep"), None),
        P("ep", None, "rep"),
        P("ep", None, "rep"),
        P("ep", "rep", None),
    )
    return jax.shard_map(shards, mesh=mesh, in_specs=in_specs, out_specs=out_specs, check_vma=False)
```

profile of v0, /device:TPU:97, one launch (start us, length us, event | category | flops | bytes accessed | tf_op | source)
XLA Modules:
  0.0 455.2 jit_solution(3262938703385457965)
XLA Ops:
  7.2 0.0 all-gather.6.cloned.1.call-start
  7.2 0.8 fusion.36
  8.1 0.2 reduce_window_sum.11
  8.3 0.8 select_reduce_fusion
  9.1 0.7 fusion.37
  9.8 4.3 scatter_custom_fusion.2
  14.1 4.1 reshape.110
  18.2 60.0 %all_to_all.37 = bf16[64,4,4096]{2,1,0:T(4,128)(2,1)S(1)} all-to-all(bf16[64,4,4096]{2,1,0:T(4,128)(2,1)} %reshape.110), channel_id=1, replica_groups=mesh['rep'=4,'ep'=64] {'ep'}, dimensions={0} | all-to-all | bytes 4194304 | tf_op jit(solution)/shard_map/all_to_all | solution.py:33
  78.1 2.5 copy.27
  80.6 0.0 all-gather.6.cloned.1.call-update
  80.7 0.0 all-gather.4.cloned.1.call-start
  80.7 4.3 scatter_custom_fusion
  85.0 4.1 reshape.107
  89.1 57.1 %all_to_all.38 = bf16[64,4,4096]{2,1,0:T(4,128)(2,1)S(1)} all-to-all(bf16[64,4,4096]{2,1,0:T(4,128)(2,1)} %reshape.107), channel_id=1, replica_groups=mesh['rep'=4,'ep'=64] {'ep'}, dimensions={0} | all-to-all | bytes 4194304 | tf_op jit(solution)/shard_map/all_to_all | solution.py:34
  146.2 2.5 copy.24
  148.7 0.0 all-gather.4.cloned.1.call-update
  148.7 0.0 reduce-scatter.7.cloned.1.call-start
  148.7 1.6 scatter_custom_fusion.1
  150.3 0.1 all_to_all.31
  150.5 14.6 %all_to_all.39 = bf16[64,1,4]{2,1,0:T(2,128)(2,1)S(1)} all-to-all(bf16[64,1,4]{2,1,0:T(2,128)(2,1)S(1)} %all_to_all.31), channel_id=1, replica_groups=mesh['rep'=4,'ep'=64] {'ep'}, dimensions={0} | all-to-all | bytes 1024 | tf_op jit(solution)/shard_map/all_to_all | solution.py:35
  165.1 9.5 %all-gather = bf16[256,1,4]{2,1,0:T(2,128)(2,1)S(1)} all-gather(bf16[64,1,4]{2,1,0:T(2,128)(2,1)S(1)} %all_to_all.39), channel_id=2, replica_groups=mesh['rep'=4,'ep'=64] {'rep'}, dimensions={0}, use_global_device_ids=true | all-gather | bytes 2560 | tf_op jit(solution)/shard_map/all_gather | solution.py:40
  174.5 0.1 convert_element_type.81
  174.7 0.1 copy.26
  174.8 7.2 %fusion.21 = f32[256,1,4,192]{0,3,2,1:T(8,128)} fusion(bf16[256,4,4096]{2,0,1:T(8,128)(2,1)} %all-gather.6.cloned.1.call-done, bf16[1,4096,192]{1,2,0:T(8,128)(2,1)S(1)} %copy-done.3), kind=kOutput, calls=%fused_computation.28 | convolution fusion | flops 1610612736 | bytes 10747904 | tf_op jit(solution)/shard_map/secd,edh->sech/dot_general | solution.py:46
  181.9 72.2 %all-gather.4.cloned.1.call-done = bf16[256,4,4096]{2,0,1:T(8,128)(2,1)} async-done(((bf16[64,4,4096]{2,0,1:T(8,128)(2,1)}), bf16[256,4,4096]{2,0,1:T(8,128)(2,1)}) %all-gather.4.cloned.1.call-update) | async-done | bytes 8388624 | tf_op jit(solution)/shard_map/all_gather | solution.py:39
  254.1 6.8 %fusion.18 = f32[256,1,4,192]{0,3,2,1:T(8,128)S(1)} fusion(bf16[256,4,4096]{2,0,1:T(8,128)(2,1)} %all-gather.4.cloned.1.call-done, bf16[1,192,4096]{2,1,0:T(8,128)(2,1)} %param.13), kind=kOutput, calls=%fused_computation.27 | convolution fusion | flops 1610612736 | bytes 10747904 | tf_op jit(solution)/shard_map/secd,ehd->sech/dot_general | solution.py:50
  261.0 4.1 multiply_reduce_fusion
  265.1 0.8 copy.31
  265.9 0.0 reduce-scatter.7.cloned.1.call-update
  265.9 0.0 reduce-scatter.5.cloned.1.call-start
  265.9 9.1 %fusion.9 = f32[256,4,4096]{2,0,1:T(8,128)} fusion(bf16[1,4096,192]{1,2,0:T(8,128)(2,1)S(1)} %copy-done, bf16[256,1,4,192]{0,3,2,1:T(8,128)(2,1)} %get-tuple-element.7), kind=kOutput, calls=%fused_computation.18 | convolution fusion | flops 1610612736 | bytes 18743296 | tf_op jit(solution)/shard_map/sech,edh->secd/dot_general | solution.py:69
  275.0 11.4 %add_convert_fusion = bf16[256,4,4096]{2,0,1:T(8,128)(2,1)} fusion(f32[256,4,4096]{2,0,1:T(8,128)} %fusion.9, bf16[256,4,192]{0,2,1:T(8,128)(2,1)S(1)} %get-tuple-element.8, bf16[1,4096,192]{1,2,0:T(8,128)(2,1)S(1)} %copy-done.3), kind=kOutput, calls=%fused_computation.6 | convolution fusion | flops 1619001344 | bytes 27131904 | tf_op jit(solution)/shard_map/sech,edh->secd/dot_general | solution.py:70
  286.5 1.2 reduce-scatter.7.cloned.1.call-done
  287.6 0.8 copy.32
  288.4 0.7 copy.29
  289.2 13.1 %all-to-all-start.4 = ((bf16[64,1,4]{2,1,0:T(2,128)(2,1)}), bf16[64,1,4]{2,1,0:T(2,128)(2,1)S(1)}, u32[]{:S(2)}, u32[]{:S(2)}) async-start(bf16[64,1,4]{2,1,0:T(2,128)(2,1)} %copy.29), calls=%async_computation.5 | async-start | bytes 65536 | tf_op jit(solution)/shard_map/all_to_all | solution.py:83
  302.2 73.2 %reduce-scatter.5.cloned.1.call-done = bf16[64,4,4096]{2,0,1:T(8,128)(2,1)} async-done(((bf16[256,4,4096]{2,0,1:T(8,128)(2,1)}), bf16[64,4,4096]{2,0,1:T(8,128)(2,1)}) %reduce-scatter.5.cloned.1.call-update) | async-done | bytes 2097168 | tf_op jit(solution)/shard_map/reduce_scatter | solution.py:76
  375.4 4.5 copy.28
  379.9 10.9 %all-to-all-start.3 = ((bf16[64,4,4096]{2,1,0:T(4,128)(2,1)}), bf16[64,4,4096]{2,1,0:T(4,128)(2,1)}, u32[]{:S(2)}, u32[]{:S(2)}) async-start(bf16[64,4,4096]{2,1,0:T(4,128)(2,1)} %copy.28), calls=%async_computation.4 | async-start | bytes 4194304 | tf_op jit(solution)/shard_map/all_to_all | solution.py:82
  390.9 6.5 %fusion.7 = bf16[1,4096,192]{1,2,0:T(8,128)(2,1)} fusion(bf16[256,4,4096]{2,0,1:T(8,128)(2,1)} %all-gather.6.cloned.1.call-done, bf16[256,1,4,192]{0,3,2,1:T(8,128)(2,1)S(1)} %copy-done.4), kind=kOutput, calls=%fused_computation.16 | convolution fusion | flops 1611399168 | bytes 10354688 | tf_op jit(solution)/shard_map/secd,sech->edh/dot_general | solution.py:63
  397.3 6.5 %fusion.6 = bf16[1,4096,192]{1,2,0:T(8,128)(2,1)} fusion(bf16[256,4,192]{0,2,1:T(8,128)(2,1)S(1)} %get-tuple-element.8, bf16[256,4,4096]{2,0,1:T(8,128)(2,1)} %all-gather.6.cloned.1.call-done), kind=kOutput, calls=%fused_computation.15 | convolution fusion | flops 1611399168 | bytes 10354688 | tf_op jit(solution)/shard_map/secd,sech->edh/dot_general | solution.py:66
  403.8 3.3 fusion.8
  407.1 0.1 reduce.1
  407.2 0.1 reshape.116
  407.3 1.7 gather_fusion.1
  409.0 30.5 %all-to-all-done.3 = bf16[64,4,4096]{2,1,0:T(4,128)(2,1)} async-done(((bf16[64,4,4096]{2,1,0:T(4,128)(2,1)}), bf16[64,4,4096]{2,1,0:T(4,128)(2,1)}, u32[]{:S(2)}, u32[]{:S(2)}) %all-to-all-start.3) | async-done | bytes 2097184 | tf_op jit(solution)/shard_map/all_to_all | solution.py:82
  439.6 3.9 reshape.115
  443.5 5.2 %gather_fusion = bf16[128,4096]{1,0:T(8,128)(2,1)} fusion(bf16[256,4096]{1,0:T(8,128)(2,1)} %reshape.115, s32[1024]{0:T(1024)S(1)} %pad_clamp_fusion), kind=kCustom, calls=%fused_computation | custom fusion | bytes 2097664 | tf_op jit(solution)/shard_map/gather | solution.py:85
  (23 shorter events, 0.1 us)
Async XLA Ops:
  7.2 253.8 %copy-start = (bf16[1,4096,192]{1,2,0:T(8,128)(2,1)S(1)}, bf16[1,4096,192]{1,2,0:T(8,128)(2,1)}, u32[]{:S(2)}) copy-start(bf16[1,4096,192]{1,2,0:T(8,128)(2,1)} %param.11) | copy-start | bytes 4718596
  7.2 167.6 %all-gather.6.cloned.1.call-start = ((), (), s32[]{:S(2)}) async-start(), calls=%async_computation.8 | async-start | bytes 10485760 | tf_op jit(solution)/shard_map/all_gather | solution.py:38
  80.7 173.5 %all-gather.4.cloned.1.call-start = ((), (), s32[]{:S(2)}) async-start(), calls=%async_computation.7 | async-start | bytes 10485760 | tf_op jit(solution)/shard_map/all_gather | solution.py:39
  148.7 26.1 %copy-start.3 = (bf16[1,4096,192]{1,2,0:T(8,128)(2,1)S(1)}, bf16[1,4096,192]{1,2,0:T(8,128)(2,1)}, u32[]{:S(2)}) copy-start(bf16[1,4096,192]{1,2,0:T(8,128)(2,1)} %param.12) | copy-start | bytes 4718596
  148.7 139.0 %reduce-scatter.7.cloned.1.call-start = ((), (), s32[]{:S(2)}) async-start(), calls=%async_computation.10 | async-start | bytes 81920
  254.1 6.9 %copy-start.2 = (bf16[256,4,4096]{2,0,1:T(8,128)(2,1)S(1)}, bf16[256,4,4096]{2,0,1:T(8,128)(2,1)}, u32[]{:S(2)}) copy-start(bf16[256,4,4096]{2,0,1:T(8,128)(2,1)} %all-gather.6.cloned.1.call-done) | copy-start | bytes 25165828
  254.1 6.9 %copy-start.5 = (f32[256,1,4,192]{0,3,2,1:T(8,128)S(1)}, f32[256,1,4,192]{0,3,2,1:T(8,128)}, u32[]{:S(2)}) copy-start(f32[256,1,4,192]{0,3,2,1:T(8,128)} %fusion.21) | copy-start | bytes 2359300
  265.9 109.5 %reduce-scatter.5.cloned.1.call-start = ((), (), s32[]{:S(2)}) async-start(), calls=%async_computation.9 | async-start | bytes 10485760 | tf_op jit(solution)/shard_map/reduce_scatter | solution.py:76
  289.2 90.7 %all-to-all-start.4 = ((bf16[64,1,4]{2,1,0:T(2,128)(2,1)}), bf16[64,1,4]{2,1,0:T(2,128)(2,1)S(1)}, u32[]{:S(2)}, u32[]{:S(2)}) async-start(bf16[64,1,4]{2,1,0:T(2,128)(2,1)} %copy.29), calls=%async_computation.5 | async-start | bytes 65536 | tf_op jit(solution)/shard_map/all_to_all | solution.py:83
  379.9 10.9 %copy-start.4 = (bf16[256,1,4,192]{0,3,2,1:T(8,128)(2,1)S(1)}, bf16[256,1,4,192]{0,3,2,1:T(8,128)(2,1)}, u32[]{:S(2)}) copy-start(bf16[256,1,4,192]{0,3,2,1:T(8,128)(2,1)} %get-tuple-element.7) | copy-start | bytes 1179652
  379.9 59.6 %all-to-all-start.3 = ((bf16[64,4,4096]{2,1,0:T(4,128)(2,1)}), bf16[64,4,4096]{2,1,0:T(4,128)(2,1)}, u32[]{:S(2)}, u32[]{:S(2)}) async-start(bf16[64,4,4096]{2,1,0:T(4,128)(2,1)} %copy.28), calls=%async_computation.4 | async-start | bytes 4194304 | tf_op jit(solution)/shard_map/all_to_all | solution.py:82
  390.8 13.0 %slice-start = ((s8[8388608]{0:T(1024)(128)(4,1)}), s8[4194304]{0:T(1024)(128)(4,1)S(1)}, s32[]{:S(2)}) async-start(s8[8388608]{0:T(1024)(128)(4,1)} %bitcast.105), calls=%async_computation.11 | async-start | bytes 8388608
  397.3 6.5 %slice-start.1 = ((s8[8388608]{0:T(1024)(128)(4,1)}), s8[4194304]{0:T(1024)(128)(4,1)S(1)}, s32[]{:S(2)}) async-start(s8[8388608]{0:T(1024)(128)(4,1)} %bitcast.105), calls=%async_computation.12 | async-start | bytes 8388608
  397.3 6.5 %copy-start.6 = (bf16[256,1,4,192]{0,3,2,1:T(8,128)(2,1)S(1)}, bf16[256,1,4,192]{0,3,2,1:T(8,128)(2,1)}, u32[]{:S(2)}) copy-start(bf16[256,1,4,192]{0,3,2,1:T(8,128)(2,1)} %get-tuple-element.6) | copy-start | bytes 1179652
  443.5 5.2 %copy-start.1 = (bf16[1,4096,192]{1,2,0:T(8,128)(2,1)S(1)}, bf16[1,4096,192]{1,2,0:T(8,128)(2,1)}, u32[]{:S(2)}) copy-start(bf16[1,4096,192]{1,2,0:T(8,128)(2,1)} %param.11) | copy-start | bytes 4718596
Sparse Core Ops, SparseCore 0:
  80.8 84.6 all-gather.5
  167.2 86.8 all-gather.3
  266.0 21.5 reduce-scatter.6
  290.3 85.0 reduce-scatter.4
where the time goes:
time: 461 us; the launch traced here: 455 us
  waiting for transfers between devices  177 us (38%)
  blocking collectives  141 us (31%)
  matrix products  54.9 us (12%)
  local copies, waits for them, and re-layouts  41.4 us (9%)
  starting transfers between devices  24.1 us (5%)
  between operations  13.9 us (3%)
    reduce_scatter x1, waiting for transfers between devices, shards(): lax.psum_scatter(part, 'rep', scatter_dimension=0, tiled=True)  73.2 us
    all_gather x1, waiting for transfers between devices, shards(): lax.all_gather(cotan_recv, 'rep', axis=0, tiled=True)  72.2 us
    all_to_all x1, blocking collectives, shards(): lax.all_to_all(input_buf, 'ep', split_axis=0, concat_axis=0, tiled=True)  60 us
    all_to_all x1, blocking collectives, shards(): lax.all_to_all(cotan_buf, 'ep', split_axis=0, concat_axis=0, tiled=True)  57.1 us
    all_to_all x1, waiting for transfers between devices, shards(): lax.all_to_all(row_grad, 'ep', split_axis=0, concat_axis=0, tiled=True)  30.5 us
    all_to_all x1, blocking collectives, shards(): lax.all_to_all(weight_buf, 'ep', split_axis=0, concat_axis=0, tiled=True)  14.6 us
    all_to_all x1, starting transfers between devices, shards(): lax.all_to_all(gate_total, 'ep', split_axis=0, concat_axis=0, tiled=True)  13.1 us
    dot_general x1, matrix products, shards(): jnp.einsum('sech,edh->secd', up_grad, up_weight, preferred_element_type=j...  11.4 us
  transfers between devices with their start and end apart: 6, of which 4 were waited for; matrix products, arithmetic and copies ran while one was open for 14% of the time, Pallas kernels for 0%

commit v1 on v0

v1 whole, which is shorter than its diff:
```python
import functools

import jax
import jax.numpy as jnp
from jax import lax
from jax.experimental import pallas as pl
from jax.experimental.pallas import tpu as pltpu
from jax.sharding import PartitionSpec as P

MESH = pl.DeviceIdType.MESH
F32, BF16 = jnp.float32, jnp.bfloat16

DZ = (0, 1, 2, 6, 3, 5, 4, 7)
NC = 8
NM = 8
CAP = 4
NQ = 4
RB = NM * NQ * CAP
HR = RB // 2
QW = 1024
HID = 192
SLOTS = 3


def pick(index, table):
    return sum(jnp.where(index == k, v, 0) for k, v in enumerate(table) if v)


def kernel(
    tok_ref, cot_ref, ids_ref, g_ref, wg_ref, wu_ref, wd_ref,
    tgrad_ref, ggrad_ref, dg_ref, du_ref, dd_ref,
    land, pack, stack, perm, wnat, wtr, part, transit, full, gpart, grecv, ret, back, acts, dout,
    a2a_s, a2a_r, ag1_s, ag1_r, ag2_s, ag2_r, rs1_s, rs1_r, rs2_s, rs2_r, gt_s, gt_r, ret_s, ret_r, w_sem, o_sem,
):
    rep, ep = lax.axis_index("rep"), lax.axis_index("ep")
    my_y, my_z, my_c = ep // 16, (ep // 2) % 8, ep % 2
    right, left, across = (rep + 1) % 4, (rep + 3) % 4, (rep + 2) % 4

    loads = [
        pltpu.make_async_copy(src.at[0], wnat.at[k], w_sem.at[k])
        for k, src in enumerate((wg_ref, wu_ref, wd_ref))
    ]
    for load in loads:
        load.start()

    barrier = pltpu.get_barrier_semaphore()

    def greet(k, carry):
        pl.semaphore_signal(barrier, inc=1, device_id=(rep, (ep + k) % 64), device_id_type=MESH)
        return carry

    lax.fori_loop(1, 64, greet, 0)
    for peer in (left, right, across):
        pl.semaphore_signal(barrier, inc=1, device_id=(peer, ep), device_id_type=MESH)

    ids = ids_ref[...].astype(F32)
    by_lane = jnp.broadcast_to(ids, (128, 128))
    by_row = by_lane.T
    a = lax.broadcasted_iota(jnp.int32, (128, 128), 0)
    b = lax.broadcasted_iota(jnp.int32, (128, 128), 1)
    same = jnp.where(by_lane == by_row, 1, 0)
    rank = jnp.sum(jnp.where(a < b, same, 0), axis=0, keepdims=True)
    expert = ids_ref[...]
    dy = ((expert >> 4) - my_y) & 3
    dz = (((expert >> 1) & 7) - my_z) & 7
    dc = (expert - my_c) & 1
    chunk_of = sum(jnp.where(dz == d, k, 0) for k, d in enumerate(DZ) if k)
    pos = (chunk_of * NM + dy * 2 + dc) * CAP + rank

    gates_row = g_ref[...].astype(F32)
    gates_col = jnp.broadcast_to(gates_row, (128, 128)).T[:, :1]
    for q in range(NQ):
        stack[0, q * 128 : (q + 1) * 128, :] = tok_ref[:, q * QW : (q + 1) * QW]
        cot = cot_ref[:, q * QW : (q + 1) * QW].astype(F32)
        stack[1, q * 128 : (q + 1) * 128, :] = (cot * gates_col).astype(BF16)

    pr = lax.broadcasted_iota(jnp.int32, (256, 256), 0)
    pc = lax.broadcasted_iota(jnp.int32, (256, 256), 1)
    perm[0] = jnp.where(pc == ((pr & 63) >> 2) * 16 + (pr >> 6) * 4 + (pr & 3), 1.0, 0.0).astype(BF16)
    perm[1] = jnp.where(pr == ((pc & 63) >> 2) * 16 + (pc >> 6) * 4 + (pc & 3), 1.0, 0.0).astype(BF16)

    def partner(c, m, sign):
        z = (my_z + sign * pick(c, DZ) + 8) % 8
        y = (my_y + sign * (m // 2) + 4) % 4
        return y * 16 + z * 2 + (my_c + m) % 2

    sr = lax.broadcasted_iota(jnp.int32, (RB, 512), 0)
    sc = lax.broadcasted_iota(jnp.int32, (RB, 512), 1)
    slot_of_row = (sr >> 4) * CAP + (sr & 3)
    quarter_ok = ((sr >> 2) & 3) == (sc >> 7)
    pos4 = jnp.concatenate([pos] * NQ, axis=1)

    def fill(c):
        onehot = jnp.where(quarter_ok & (pos4 - c * (NM * CAP) == slot_of_row), 1.0, 0.0).astype(BF16)
        for k in range(2):
            pack[k, c] = jnp.dot(onehot, stack[k], preferred_element_type=F32).astype(BF16)

    def send(c, m):
        rows = pl.ds(pl.multiple_of(m * 16, 16), 16)
        for k in range(2):
            pltpu.make_async_remote_copy(
                src_ref=pack.at[k, c, rows],
                dst_ref=land.at[k, c, 0, rows],
                send_sem=a2a_s.at[k, c],
                recv_sem=a2a_r.at[k, c],
                device_id=(rep, partner(c, m, 1)),
                device_id_type=MESH,
            ).start()

    fill(0)
    pl.semaphore_wait(barrier, 66)
    own_copies = [
        pltpu.make_async_copy(pack.at[k, 0, pl.ds(0, 16)], land.at[k, 0, 0, pl.ds(0, 16)], a2a_r.at[k, 0])
        for k in range(2)
    ]
    for copy in own_copies:
        copy.start()

    def send_first(m, carry):
        send(0, m)
        return carry

    lax.fori_loop(1, NM, send_first, 0)

    def send_chunk(c, carry):
        fill(c)

        def one(m, inner):
            send(c, m)
            return inner

        lax.fori_loop(0, NM, one, 0)
        return carry

    lax.fori_loop(1, NC, send_chunk, 0)

    for load in loads:
        load.wait()

    def turn(j, carry):
        cols = pl.ds(pl.multiple_of(j * 512, 512), 512)
        for k in range(3):
            wtr[k, cols, :] = wnat[k, :, cols].T
        return carry

    lax.fori_loop(0, 8, turn, 0)

    def ring(src, dst, send_sem, recv_sem, peer):
        return pltpu.make_async_remote_copy(
            src_ref=src, dst_ref=dst, send_sem=send_sem, recv_sem=recv_sem,
            device_id=(peer, ep), device_id_type=MESH,
        )

    def gather_one(k, c):
        own = land.at[k, c, 0, pl.ds(0, RB)]
        return (
            ring(own, land.at[k, c, 0, pl.ds(RB, RB)], ag1_s.at[k, 0, c], ag1_r.at[k, 0, c], right),
            ring(own, land.at[k, c, 1, pl.ds(0, RB)], ag1_s.at[k, 1, c], ag1_r.at[k, 1, c], left),
        )

    def gather_two(k, c):
        return (
            ring(
                land.at[k, c, 0, pl.ds(RB, HR)], land.at[k, c, 1, pl.ds(RB, HR)],
                ag2_s.at[k, 0, c], ag2_r.at[k, 0, c], right,
            ),
            ring(
                land.at[k, c, 1, pl.ds(HR, HR)], land.at[k, c, 1, pl.ds(RB + HR, HR)],
                ag2_s.at[k, 1, c], ag2_r.at[k, 1, c], left,
            ),
        )

    def scatter_one(c):
        p = c % SLOTS
        return (
            ring(part.at[p, 3, pl.ds(0, HR)], transit.at[0, c], rs1_s.at[0, c], rs1_r.at[0, c], right),
            ring(part.at[p, 3, pl.ds(HR, HR)], transit.at[1, c], rs1_s.at[1, c], rs1_r.at[1, c], left),
        )

    def scatter_two(c):
        p = c % SLOTS
        return (
            ring(part.at[p, 2], full.at[0, c], rs2_s.at[0, c], rs2_r.at[0, c], right),
            ring(part.at[p, 1], full.at[1, c], rs2_s.at[1, c], rs2_r.at[1, c], left),
        )

    def gate_copies(c):
        return [
            ring(gpart.at[c], grecv.at[j, c], gt_s.at[j, c], gt_r.at[j, c], peer)
            for j, peer in enumerate((right, left, across))
        ]

    def step_gather_one(c):
        for k in range(2):
            whole = land.at[k, c, 0, pl.ds(0, RB)]
            pltpu.make_async_copy(whole, whole, a2a_r.at[k, c]).wait()
            for copy in gather_one(k, c):
                copy.start()

    def step_gather_two(c):
        for k in range(2):
            firsts, seconds = gather_one(k, c), gather_two(k, c)
            for first, second in zip(firsts, seconds):
                first.wait_recv()
                second.start()

    def step_compute(c):
        p = c % SLOTS
        for k in range(2):
            for copy in gather_two(k, c):
                copy.wait_recv()
                copy.wait_send()
            for copy in gather_one(k, c):
                copy.wait_send()
        rows = []
        for k in range(2):
            for g in range(2):
                land[k, c, g] = jnp.dot(perm[0], land[k, c, g], preferred_element_type=F32).astype(BF16)

        def quarter(k, q):
            return jnp.concatenate([land[k, c, g, q * 64 : (q + 1) * 64, :] for g in range(2)], axis=0)

        def project(k, w):
            return sum(
                jnp.dot(quarter(k, q), wtr[w, q * QW : (q + 1) * QW, :], preferred_element_type=F32)
                for q in range(NQ)
            )

        gate_pre, up_pre, weighted = project(0, 0), project(0, 1), project(1, 2)
        logistic = jax.nn.sigmoid(gate_pre)
        activated = gate_pre * logistic
        hidden = (activated * up_pre).astype(BF16)
        pre_grad = (weighted * up_pre * logistic * (1.0 + gate_pre * (1.0 - logistic))).astype(BF16)
        up_grad = (weighted * activated).astype(BF16)
        gate_sum = jnp.sum(hidden.astype(F32) * weighted, axis=1, keepdims=True)
        gpart[c] = jnp.broadcast_to(gate_sum, (128, 128)).T[:8, :]
        cols = pl.ds(pl.multiple_of(c * 128, 128), 128)
        acts[0, :, cols] = pre_grad.T
        acts[1, :, cols] = up_grad.T
        acts[2, :, cols] = hidden.T
        for copy in gate_copies(c):
            copy.start()
        parts = []
        for q in range(NQ):
            both = jnp.dot(pre_grad, wnat[0, :, q * QW : (q + 1) * QW], preferred_element_type=F32)
            both = both + jnp.dot(up_grad, wnat[1, :, q * QW : (q + 1) * QW], preferred_element_type=F32)
            parts.append(both.astype(BF16))
        for g in (1, 0):
            stacked = jnp.concatenate([piece[g * 64 : (g + 1) * 64] for piece in parts], axis=0)
            message = jnp.dot(perm[1], stacked, preferred_element_type=F32).astype(BF16)
            part[p, 2 * g] = message[:RB]
            part[p, 2 * g + 1] = message[RB:]
        for copy in scatter_one(c):
            copy.start()

    def step_scatter_two(c):
        p = c % SLOTS
        ones, twos = scatter_one(c), scatter_two(c)
        for j, (rel, rows) in enumerate(((2, pl.ds(0, HR)), (1, pl.ds(HR, HR)))):
            ones[j].wait_recv()
            total = part[p, rel, rows, :].astype(F32) + transit[j, c].astype(F32)
            part[p, rel, rows, :] = total.astype(BF16)
            twos[j].start()

    gr = lax.broadcasted_iota(jnp.int32, (RB, 128), 0)
    gl = lax.broadcasted_iota(jnp.int32, (RB, 128), 1)
    slot_lane = (gr >> 4) * CAP + (gr & 3)

    def ret_copy(c, m):
        rows = pl.ds(pl.multiple_of(m * 16, 16), 16)
        return pltpu.make_async_remote_copy(
            src_ref=ret.at[c, rows],
            dst_ref=back.at[c, rows],
            send_sem=ret_s.at[c],
            recv_sem=ret_r.at[c],
            device_id=(rep, partner(c, m, -1)),
            device_id_type=MESH,
        )

    def step_return(c):
        p = c % SLOTS
        for copy in scatter_two(c):
            copy.wait_recv()
            copy.wait_send()
        for copy in scatter_one(c):
            copy.wait_send()
        for copy in gate_copies(c):
            copy.wait()
        total = part[p, 0].astype(F32) + full[0, c].astype(F32) + full[1, c].astype(F32)
        ret[c, :, :QW] = total.astype(BF16)
        gate = jnp.where(gl == slot_lane, gpart[c, :1, :], 0.0)
        gate = gate + jnp.where(gl == slot_lane + 64, grecv[0, c, :1, :], 0.0)
        gate = gate + jnp.where(gl == slot_lane + 32, grecv[1, c, :1, :], 0.0)
        gate = gate + jnp.where(gl == slot_lane + 96, grecv[2, c, :1, :], 0.0)
        gate = jnp.sum(gate, axis=1, keepdims=True)
        ret[c, :, QW:] = jnp.broadcast_to(gate, (RB, 128)).astype(BF16)

        @pl.when(c == 0)
        def _():
            pltpu.make_async_copy(ret.at[0, pl.ds(0, 16)], back.at[0, pl.ds(0, 16)], ret_r.at[0]).start()

        def one(m, carry):
            ret_copy(c, m).start()
            return carry

        lax.fori_loop(jnp.where(c == 0, 1, 0), NM, one, 0)

    def step(t, carry):
        pl.when(t < NC)(lambda: step_gather_one(t))
        pl.when((t >= 1) & (t < NC + 1))(lambda: step_gather_two(t - 1))
        pl.when((t >= 2) & (t < NC + 2))(lambda: step_compute(t - 2))
        pl.when((t >= 3) & (t < NC + 3))(lambda: step_scatter_two(t - 3))
        pl.when((t >= 4) & (t < NC + 4))(lambda: step_return(t - 4))
        return carry

    lax.fori_loop(0, NC + 4, step, 0)

    def weight_grads(j, carry):
        q, col = j // 4, pl.ds(pl.multiple_of((j % 4) * 256, 256), 256)
        out = pl.ds(pl.multiple_of(j * 256, 256), 256)
        rows = pl.ds(pl.multiple_of(q * 64, 64), 64)
        x = land[0, :, :, rows, col].reshape(NC * 128, 256)
        cot = land[1, :, :, rows, col].reshape(NC * 128, 256)
        dout[0, :, out] = jnp.dot(acts[0], x, preferred_element_type=F32).astype(BF16)
        dout[1, :, out] = jnp.dot(acts[1], x, preferred_element_type=F32).astype(BF16)
        dout[2, :, out] = jnp.dot(acts[2], cot, preferred_element_type=F32).astype(BF16)
        return carry

    lax.fori_loop(0, 16, weight_grads, 0)
    stores = [
        pltpu.make_async_copy(dout.at[k], dst.at[0], o_sem.at[k])
        for k, dst in enumerate((dg_ref, du_ref, dd_ref))
    ]
    for store in stores:
        store.start()

    pos_col = jnp.broadcast_to(pos.astype(F32), (128, 128)).T[:, :1].astype(jnp.int32)
    mr = lax.broadcasted_iota(jnp.int32, (128, NC * RB), 1)
    hit = (mr >> 4) * CAP + (mr & 3) == pos_col
    for c in range(NC):
        pltpu.make_async_copy(back.at[c], back.at[c], ret_r.at[c]).wait()
    rows_back = back[...].reshape(NC * RB, QW + 128)
    for q in range(NQ):
        take = jnp.where(hit & (((mr >> 2) & 3) == q), 1.0, 0.0).astype(BF16)
        tgrad_ref[:, q * QW : (q + 1) * QW] = jnp.dot(
            take, rows_back[:, :QW], preferred_element_type=F32
        ).astype(BF16)
        if q == 0:
            gate = jnp.dot(take, rows_back[:, QW:], preferred_element_type=F32)
            ggrad_ref[...] = (gate.T[:1, :] / gates_row).astype(BF16)

    skip = pl.ds(16, RB - 16)
    for c in range(NC):
        rows = skip if c == 0 else pl.ds(0, RB)
        for k in range(2):
            pltpu.make_async_copy(pack.at[k, c, rows], pack.at[k, c, rows], a2a_s.at[k, c]).wait()
        pltpu.make_async_copy(ret.at[c, rows], ret.at[c, rows], ret_s.at[c]).wait()
    for store in stores:
        store.wait()


def shards(tokens, cotangent, expert_ids, gates, gate_weight, up_weight, down_weight):
    rows, width = tokens.shape
    vmem, hbm = pl.BlockSpec(memory_space=pltpu.VMEM), pl.BlockSpec(memory_space=pl.ANY)
    dma = pltpu.SemaphoreType.DMA
    out = pl.pallas_call(
        kernel,
        out_shape=(
            jax.ShapeDtypeStruct((rows, width), BF16),
            jax.ShapeDtypeStruct((1, rows), BF16),
            jax.ShapeDtypeStruct((1, HID, width), BF16),
            jax.ShapeDtypeStruct((1, HID, width), BF16),
            jax.ShapeDtypeStruct((1, HID, width), BF16),
        ),
        in_specs=[vmem] * 4 + [hbm] * 3,
        out_specs=(vmem, vmem, hbm, hbm, hbm),
        scratch_shapes=[
            pltpu.VMEM((2, NC, 2, 2 * RB, QW), BF16),
            pltpu.VMEM((2, NC, RB, QW), BF16),
            pltpu.VMEM((2, NQ * 128, QW), BF16),
            pltpu.VMEM((2, 256, 256), BF16),
            pltpu.VMEM((3, HID, width), BF16),
            pltpu.VMEM((3, width, HID), BF16),
            pltpu.VMEM((SLOTS, 4, RB, QW), BF16),
            pltpu.VMEM((2, NC, HR, QW), BF16),
            pltpu.VMEM((2, NC, RB, QW), BF16),
            pltpu.VMEM((NC, 8, 128), F32),
            pltpu.VMEM((3, NC, 8, 128), F32),
            pltpu.VMEM((NC, RB, QW + 128), BF16),
            pltpu.VMEM((NC, RB, QW + 128), BF16),
            pltpu.VMEM((3, HID, NC * 128), BF16),
            pltpu.VMEM((3, HID, width), BF16),
            dma((2, NC)), dma((2, NC)),
            dma((2, 2, NC)), dma((2, 2, NC)), dma((2, 2, NC)), dma((2, 2, NC)),
            dma((2, NC)), dma((2, NC)), dma((2, NC)), dma((2, NC)),
            dma((3, NC)), dma((3, NC)),
            dma((NC,)), dma((NC,)),
            dma((3,)), dma((3,)),
        ],
        compiler_params=pltpu.CompilerParams(
            collective_id=0, has_side_effects=True, vmem_limit_bytes=62 * 1024 * 1024
        ),
    )(
        tokens,
        cotangent,
        expert_ids.reshape(1, rows),
        gates.reshape(1, rows),
        jnp.transpose(gate_weight, (0, 2, 1)),
        jnp.transpose(up_weight, (0, 2, 1)),
        down_weight,
    )
    token_grad, gates_grad, gate_grad, upper_grad, down_grad = out
    return (
        token_grad,
        gates_grad.reshape(rows, 1),
        jnp.transpose(gate_grad, (0, 2, 1)),
        jnp.transpose(upper_grad, (0, 2, 1)),
        down_grad,
    )


def solution(mesh):
    in_specs = (
        P(("rep", "ep"), None),
        P(("rep", "ep"), None),
        P(("rep", "ep"), None),
        P(("rep", "ep"), None),
        P("ep", None, "rep"),
        P("ep", None, "rep"),
        P("ep", "rep", None),
    )
    out_specs = (
        P(("rep", "ep"), None),
        P(("rep", "ep"), None),
        P("ep", None, "rep"),
        P("ep", None, "rep"),
        P("ep", "rep", None),
    )
    return jax.shard_map(shards, mesh=mesh, in_specs=in_specs, out_specs=out_specs, check_vma=False)
```

time: 461 us -> 274 us (0.59)
  Pallas kernels: 0 us -> 261 us
  waiting for transfers between devices: 177 us -> 0 us
  blocking collectives: 141 us -> 0 us
  matrix products: 54.9 us -> 0 us
  local copies, waits for them, and re-layouts: 41.4 us -> 8.02 us
  starting transfers between devices: 24.1 us -> 0 us
  between operations: 13.9 us -> 0.66 us
    pallas_call x0 -> x1, Pallas kernels: none -> 261 us  [shards(): pl.pallas_call(kernel, out_shape=(jax.ShapeDtypeStruct((rows, width), BF1...]
    all_to_all x3 -> x0, blocking collectives: 132 us -> none  [the longest x1 60 us: shards(): lax.all_to_all(input_buf, 'ep', split_axis=0, concat_axis=0, tiled=True)]
    reduce_scatter x1 -> x0, waiting for transfers between devices: 73.2 us -> none  [shards(): lax.psum_scatter(part, 'rep', scatter_dimension=0, tiled=True)]
    all_gather x2 -> x0, waiting for transfers between devices: 72.2 us -> none  [the longest x1 72.2 us: shards(): lax.all_gather(cotan_recv, 'rep', axis=0, tiled=True)]
    dot_general x8 -> x0, matrix products: 54.9 us -> none  [the longest x1 11.4 us: shards(): jnp.einsum('sech,edh->secd', up_grad, up_weight, preferred_element_type=j...]
    all_to_all x2 -> x0, waiting for transfers between devices: 30.5 us -> none  [the longest x1 30.5 us: shards(): lax.all_to_all(row_grad, 'ep', split_axis=0, concat_axis=0, tiled=True)]
    all_to_all x2 -> x0, starting transfers between devices: 24 us -> none  [the longest x1 13.1 us: shards(): lax.all_to_all(gate_total, 'ep', split_axis=0, concat_axis=0, tiled=True)]
    reshape x4 -> x0, local copies, waits for them, and re-layouts: 12.3 us -> none  [the longest x1 4.13 us: shards(): cotan_buf = cotan_buf.reshape(peer_count, slot_rows, width)]
  transfers between devices with their start and end apart: 6 -> 0, of which waited for: 4 -> 0; matrix products, arithmetic and copies ran while one was open for 14% -> 0% of each run, Pallas kernels for 0% -> 0%
where the time goes in v1:
time: 274 us; the launch traced here: 270 us
  Pallas kernels  261 us (95%)
  local copies, waits for them, and re-layouts  8.02 us (3%)
    pallas_call x1, Pallas kernels, shards(): pl.pallas_call(kernel, out_shape=(jax.ShapeDtypeStruct((rows, width), BF1...  261 us
    unnamed x13, local copies, waits for them, and re-layouts  8.02 us

profile of v1, /device:TPU:97, one launch (start us, length us, event | category | flops | bytes accessed | tf_op | source)
XLA Modules:
  0.0 270.0 jit_solution(10282414480992153549)
XLA Ops:
  0.6 261.3 %shard_map.110 = (bf16[128,4096]{1,0:T(8,128)(2,1)}, bf16[1,128]{1,0:T(2,128)(2,1)}, bf16[1,192,4096]{2,1,0:T(8,128)(2,1)}, bf16[1,192,4096]{2,1,0:T(8,128)(2,1)}, bf16[1,192,4096]{2,1,0:T(8,128)(2,1)}) custom-call(bf16[128,4096]{1,0:T(8,128)(2,1)} %tok_ref.1, bf16[128,4096]{1,0:T(8,128)(2,1)} %cot_ref.1, s32[1,128]{1,0:T(1,128)} %bitcast.11, ...), custom_call_target="tpu_custom_call" | custom-call | tf_op jit(solution)/shard_map/pallas_call | solution.py:366
  261.9 0.0 copy-start.3
  262.0 0.0 copy-start.2
  262.0 2.4 copy.17
  264.4 0.0 copy-done.3
  264.4 0.5 copy.18
  264.9 0.0 copy-done.2
  264.9 0.0 copy-start.1
  264.9 1.1 copy.19
  266.0 0.8 copy-done.1
  266.9 0.0 copy-start
  266.9 1.1 copy.20
  268.0 0.8 copy-done
  268.8 1.1 copy.21
Async XLA Ops:
  261.9 2.4 copy-start.3
  262.0 2.9 %copy-start.2 = (bf16[1,192,4096]{2,1,0:T(8,128)(2,1)S(1)}, bf16[1,192,4096]{2,1,0:T(8,128)(2,1)}, u32[]{:S(2)}) copy-start(bf16[1,192,4096]{2,1,0:T(8,128)(2,1)} %get-tuple-element.12) | copy-start | bytes 4718596
  264.9 2.0 copy-start.1
  266.9 2.0 copy-start

commit v2 on v1

v2 whole, which is shorter than its diff:
```python
import jax
import jax.numpy as jnp
from jax import lax
from jax.experimental import pallas as pl
from jax.experimental.pallas import tpu as pltpu
from jax.sharding import PartitionSpec as P

MESH = pl.DeviceIdType.MESH
F32, BF16 = jnp.float32, jnp.bfloat16

DZ = (0, 7, 2, 5, 4, 3, 6, 1)
NC = 16
NM = 4
CAP = 4
NQ = 4
RB = NM * NQ * CAP
HR = RB // 2
QW = 1024
BW = QW + 128
HID = 192
SLOTS = 3
ROWS = NC * NM * CAP


def pick(index, table):
    return sum(jnp.where(index == k, v, 0) for k, v in enumerate(table) if v)


def positions(ids_ref, my_y, my_z, my_c):
    ids = ids_ref[...].astype(F32)
    by_lane = jnp.broadcast_to(ids, (128, 128))
    by_row = by_lane.T
    a = lax.broadcasted_iota(jnp.int32, (128, 128), 0)
    b = lax.broadcasted_iota(jnp.int32, (128, 128), 1)
    same = jnp.where(by_lane == by_row, 1, 0)
    rank = jnp.sum(jnp.where(a < b, same, 0), axis=0, keepdims=True)
    expert = ids_ref[...]
    dy = ((expert >> 4) - my_y) & 3
    dz = (((expert >> 1) & 7) - my_z) & 7
    dc = (expert - my_c) & 1
    at_z = sum(jnp.where(dz == d, k, 0) for k, d in enumerate(DZ) if k)
    return ((at_z * 2 + dc) * NM + dy) * CAP + rank


def kernel(
    tok_ref, cot_ref, ids_ref, g_ref, wg_ref, wu_ref, wd_ref,
    back, dg_ref, du_ref, dd_ref,
    land, pack, stack, perm, wnat, wtr, part, transit, full, gpart, grecv, ret, acts, acts_t, dout,
    a2a_s, a2a_r, ag1_s, ag1_r, ag2_s, ag2_r, rs1_s, rs1_r, rs2_s, rs2_r, gt_s, gt_r, ret_s, ret_r, w_sem, o_sem,
):
    rep, ep = lax.axis_index("rep"), lax.axis_index("ep")
    my_y, my_z, my_c = ep // 16, (ep // 2) % 8, ep % 2
    right, left, across = (rep + 1) % 4, (rep + 3) % 4, (rep + 2) % 4

    loads = [
        pltpu.make_async_copy(src.at[0], wnat.at[k], w_sem.at[k])
        for k, src in enumerate((wg_ref, wu_ref, wd_ref))
    ]
    for load in loads:
        load.start()

    barrier = pltpu.get_barrier_semaphore()

    def greet(k, carry):
        pl.semaphore_signal(barrier, inc=1, device_id=(rep, (ep + k) % 64), device_id_type=MESH)
        return carry

    lax.fori_loop(1, 64, greet, 0)
    for peer in (left, right, across):
        pl.semaphore_signal(barrier, inc=1, device_id=(peer, ep), device_id_type=MESH)

    pos = positions(ids_ref, my_y, my_z, my_c)
    gates_row = g_ref[...].astype(F32)
    gates_col = jnp.broadcast_to(gates_row, (128, 128)).T[:, :1]
    for q in range(NQ):
        stack[0, q * 128 : (q + 1) * 128, :] = tok_ref[:, q * QW : (q + 1) * QW]
        cot = cot_ref[:, q * QW : (q + 1) * QW].astype(F32)
        stack[1, q * 128 : (q + 1) * 128, :] = (cot * gates_col).astype(BF16)

    pr = lax.broadcasted_iota(jnp.int32, (256, 256), 0)
    pc = lax.broadcasted_iota(jnp.int32, (256, 256), 1)
    perm[0] = jnp.where(pc == ((pr & 63) >> 2) * 16 + (pr >> 6) * 4 + (pr & 3), 1.0, 0.0).astype(BF16)
    perm[1] = jnp.where(pr == ((pc & 63) >> 2) * 16 + (pc >> 6) * 4 + (pc & 3), 1.0, 0.0).astype(BF16)

    def partner(c, m, sign):
        z = (my_z + sign * pick(c // 2, DZ) + 8) % 8
        y = (my_y + sign * m + 4) % 4
        return y * 16 + z * 2 + (my_c + c) % 2

    sr = lax.broadcasted_iota(jnp.int32, (2 * RB, 512), 0)
    sc = lax.broadcasted_iota(jnp.int32, (2 * RB, 512), 1)
    slot_of_row = (sr >> 4) * CAP + (sr & 3)
    quarter_ok = ((sr >> 2) & 3) == (sc >> 7)
    pos4 = jnp.concatenate([pos] * NQ, axis=1)

    def fill(j, carry):
        onehot = jnp.where(quarter_ok & (pos4 - j * (2 * NM * CAP) == slot_of_row), 1.0, 0.0).astype(BF16)
        for k in range(2):
            rows = jnp.dot(onehot, stack[k], preferred_element_type=F32).astype(BF16)
            pack[k, 2 * j] = rows[:RB]
            pack[k, 2 * j + 1] = rows[RB:]
        return carry

    lax.fori_loop(0, NC // 2, fill, 0)

    def send(c, m):
        rows = pl.ds(pl.multiple_of(m * 16, 16), 16)
        for k in range(2):
            pltpu.make_async_remote_copy(
                src_ref=pack.at[k, c, rows],
                dst_ref=land.at[k, c, rows],
                send_sem=a2a_s.at[k, c],
                recv_sem=a2a_r.at[k, c],
                device_id=(rep, partner(c, m, 1)),
                device_id_type=MESH,
            ).start()

    def send_chunk(c, carry):
        def one(m, inner):
            send(c, m)
            return inner

        lax.fori_loop(jnp.where(c == 0, 1, 0), NM, one, 0)
        return carry

    for load in loads:
        load.wait()

    def turn(j, carry):
        cols = pl.ds(pl.multiple_of(j * 512, 512), 512)
        for k in range(3):
            wtr[k, cols, :] = wnat[k, :, cols].T
        return carry

    lax.fori_loop(0, 8, turn, 0)

    pl.semaphore_wait(barrier, 66)
    for k in range(2):
        pltpu.make_async_copy(pack.at[k, 0, pl.ds(0, 16)], land.at[k, 0, pl.ds(0, 16)], a2a_r.at[k, 0]).start()
    lax.fori_loop(0, 4, send_chunk, 0)

    def ring(src, dst, send_sem, recv_sem, peer):
        return pltpu.make_async_remote_copy(
            src_ref=src, dst_ref=dst, send_sem=send_sem, recv_sem=recv_sem,
            device_id=(peer, ep), device_id_type=MESH,
        )

    def gather_one(k, c):
        own = land.at[k, c, pl.ds(0, RB)]
        return (
            ring(own, land.at[k, c, pl.ds(RB, RB)], ag1_s.at[k, 0, c], ag1_r.at[k, 0, c], right),
            ring(own, land.at[k, c, pl.ds(2 * RB, RB)], ag1_s.at[k, 1, c], ag1_r.at[k, 1, c], left),
        )

    def gather_two(k, c):
        return (
            ring(
                land.at[k, c, pl.ds(RB, HR)], land.at[k, c, pl.ds(3 * RB, HR)],
                ag2_s.at[k, 0, c], ag2_r.at[k, 0, c], right,
            ),
            ring(
                land.at[k, c, pl.ds(2 * RB + HR, HR)], land.at[k, c, pl.ds(3 * RB + HR, HR)],
                ag2_s.at[k, 1, c], ag2_r.at[k, 1, c], left,
            ),
        )

    def scatter_one(c):
        p = c % SLOTS
        return (
            ring(part.at[p, 3, pl.ds(0, HR)], transit.at[0, c], rs1_s.at[0, c], rs1_r.at[0, c], right),
            ring(part.at[p, 3, pl.ds(HR, HR)], transit.at[1, c], rs1_s.at[1, c], rs1_r.at[1, c], left),
        )

    def scatter_two(c):
        p = c % SLOTS
        return (
            ring(part.at[p, 2], full.at[0, c], rs2_s.at[0, c], rs2_r.at[0, c], right),
            ring(part.at[p, 1], full.at[1, c], rs2_s.at[1, c], rs2_r.at[1, c], left),
        )

    def gate_copies(c):
        return [
            ring(gpart.at[c], grecv.at[j, c], gt_s.at[j, c], gt_r.at[j, c], peer)
            for j, peer in enumerate((right, left, across))
        ]

    def step_gather_one(c):
        for k in range(2):
            whole = land.at[k, c, pl.ds(0, RB)]
            pltpu.make_async_copy(whole, whole, a2a_r.at[k, c]).wait()
            for copy in gather_one(k, c):
                copy.start()

    def step_gather_two(c):
        for k in range(2):
            firsts, seconds = gather_one(k, c), gather_two(k, c)
            for first, second in zip(firsts, seconds):
                first.wait_recv()
                second.start()

    def step_compute(c):
        p = c % SLOTS
        for k in range(2):
            for copy in gather_two(k, c):
                copy.wait_recv()
                copy.wait_send()
            for copy in gather_one(k, c):
                copy.wait_send()
        for k in range(2):
            land[k, c] = jnp.dot(perm[0], land[k, c], preferred_element_type=F32).astype(BF16)

        def project(k, w):
            return sum(
                jnp.dot(land[k, c, q * 64 : (q + 1) * 64, :], wtr[w, q * QW : (q + 1) * QW, :], preferred_element_type=F32)
                for q in range(NQ)
            )

        gate_pre, up_pre, weighted = project(0, 0), project(0, 1), project(1, 2)
        logistic = jax.nn.sigmoid(gate_pre)
        activated = gate_pre * logistic
        hidden = (activated * up_pre).astype(BF16)
        pre_grad = (weighted * up_pre * logistic * (1.0 + gate_pre * (1.0 - logistic))).astype(BF16)
        up_grad = (weighted * activated).astype(BF16)
        gate_sum = jnp.sum(hidden.astype(F32) * weighted, axis=1, keepdims=True)
        gate_sum = jnp.broadcast_to(jnp.concatenate([gate_sum, gate_sum], axis=0), (128, 128))
        gpart[c] = gate_sum.T[:8, :]
        rows = pl.ds(pl.multiple_of(c * 64, 64), 64)
        acts[0, rows, :] = pre_grad
        acts[1, rows, :] = up_grad
        acts[2, rows, :] = hidden
        for copy in gate_copies(c):
            copy.start()
        parts = []
        for q in range(NQ):
            both = jnp.dot(pre_grad, wnat[0, :, q * QW : (q + 1) * QW], preferred_element_type=F32)
            both = both + jnp.dot(up_grad, wnat[1, :, q * QW : (q + 1) * QW], preferred_element_type=F32)
            parts.append(both.astype(BF16))
        message = jnp.dot(perm[1], jnp.concatenate(parts, axis=0), preferred_element_type=F32).astype(BF16)
        for rel in range(4):
            part[p, rel] = message[rel * RB : (rel + 1) * RB]
        for copy in scatter_one(c):
            copy.start()

    def step_scatter_two(c):
        p = c % SLOTS
        ones, twos = scatter_one(c), scatter_two(c)
        for j, (rel, rows) in enumerate(((2, pl.ds(0, HR)), (1, pl.ds(HR, HR)))):
            ones[j].wait_recv()
            total = part[p, rel, rows, :].astype(F32) + transit[j, c].astype(F32)
            part[p, rel, rows, :] = total.astype(BF16)
            twos[j].start()

    gr = lax.broadcasted_iota(jnp.int32, (RB, 128), 0)
    gl = lax.broadcasted_iota(jnp.int32, (RB, 128), 1)
    slot_lane = (gr >> 4) * CAP + (gr & 3)

    def ret_copy(c, m):
        rows = pl.ds(pl.multiple_of(m * 16, 16), 16)
        return pltpu.make_async_remote_copy(
            src_ref=ret.at[c, rows],
            dst_ref=back.at[c, rows],
            send_sem=ret_s.at[c],
            recv_sem=ret_r.at[c],
            device_id=(rep, partner(c, m, -1)),
            device_id_type=MESH,
        )

    def step_return(c):
        p = c % SLOTS
        for copy in scatter_two(c):
            copy.wait_recv()
            copy.wait_send()
        for copy in scatter_one(c):
            copy.wait_send()
        for copy in gate_copies(c):
            copy.wait()
        total = part[p, 0].astype(F32) + full[0, c].astype(F32) + full[1, c].astype(F32)
        ret[c, :, :QW] = total.astype(BF16)
        gate = jnp.where(gl == slot_lane, gpart[c, :1, :], 0.0)
        gate = gate + jnp.where(gl == slot_lane + 2 * NM * CAP, grecv[0, c, :1, :], 0.0)
        gate = gate + jnp.where(gl == slot_lane + NM * CAP, grecv[1, c, :1, :], 0.0)
        gate = gate + jnp.where(gl == slot_lane + 3 * NM * CAP, grecv[2, c, :1, :], 0.0)
        gate = jnp.sum(gate, axis=1, keepdims=True)
        ret[c, :, QW:] = jnp.broadcast_to(gate, (RB, 128)).astype(BF16)

        @pl.when(c == 0)
        def _():
            pltpu.make_async_copy(ret.at[0, pl.ds(0, 16)], back.at[0, pl.ds(0, 16)], ret_r.at[0]).start()

        def one(m, carry):
            ret_copy(c, m).start()
            return carry

        lax.fori_loop(jnp.where(c == 0, 1, 0), NM, one, 0)

    def weight_grads(j, carry):
        q, col = j // 4, pl.ds(pl.multiple_of((j % 4) * 256, 256), 256)
        out = pl.ds(pl.multiple_of(j * 256, 256), 256)
        rows = pl.ds(pl.multiple_of(q * 64, 64), 64)
        x = land[0, :, rows, col].reshape(NC * 64, 256)
        cot = land[1, :, rows, col].reshape(NC * 64, 256)
        dout[0, :, out] = jnp.dot(acts_t[0], x, preferred_element_type=F32).astype(BF16)
        dout[1, :, out] = jnp.dot(acts_t[1], x, preferred_element_type=F32).astype(BF16)
        dout[2, :, out] = jnp.dot(acts_t[2], cot, preferred_element_type=F32).astype(BF16)
        return carry

    def turn_acts():
        for k in range(3):
            acts_t[k] = acts[k].T

    def step(t, carry):
        pl.when(t < NC)(lambda: step_gather_one(t))
        pl.when((t >= 1) & (t < NC + 1))(lambda: step_gather_two(t - 1))
        lax.fori_loop(jnp.where(t < 2, 4 + 6 * t, NC), jnp.where(t < 2, 10 + 6 * t, NC), send_chunk, 0)
        pl.when((t >= 2) & (t < NC + 2))(lambda: step_compute(t - 2))
        pl.when((t >= 3) & (t < NC + 3))(lambda: step_scatter_two(t - 3))
        pl.when((t >= 4) & (t < NC + 4))(lambda: step_return(t - 4))
        pl.when(t == NC + 1)(turn_acts)
        first = jnp.where(t == NC + 1, 0, jnp.where(t == NC + 2, 4, 10))
        last = jnp.where(t == NC + 1, 4, jnp.where(t == NC + 2, 10, jnp.where(t == NC + 3, 16, 0)))
        lax.fori_loop(first, last, weight_grads, 0)
        return carry

    lax.fori_loop(0, NC + 4, step, 0)

    stores = [
        pltpu.make_async_copy(dout.at[k], dst.at[0], o_sem.at[k])
        for k, dst in enumerate((dg_ref, du_ref, dd_ref))
    ]
    for store in stores:
        store.start()
    skip = pl.ds(16, RB - 16)
    for c in range(NC):
        pltpu.make_async_copy(back.at[c], back.at[c], ret_r.at[c]).wait()
        rows = skip if c == 0 else pl.ds(0, RB)
        for k in range(2):
            pltpu.make_async_copy(pack.at[k, c, rows], pack.at[k, c, rows], a2a_s.at[k, c]).wait()
        pltpu.make_async_copy(ret.at[c, rows], ret.at[c, rows], ret_s.at[c]).wait()
    for store in stores:
        store.wait()


def finish(
    back_hbm, ids_ref, g_ref, dg_ref, du_ref, dd_ref,
    tgrad_ref, ggrad_ref, og_ref, ou_ref, od_ref,
    back, grads, b_sem, in_sem, out_sem,
):
    ep = lax.axis_index("ep")
    load = pltpu.make_async_copy(back_hbm, back, b_sem)
    load.start()
    fetches = [
        pltpu.make_async_copy(src.at[0], grads.at[k], in_sem.at[k]) for k, src in enumerate((dg_ref, du_ref, dd_ref))
    ]
    stores = [
        pltpu.make_async_copy(grads.at[k], dst.at[0], out_sem.at[k]) for k, dst in enumerate((og_ref, ou_ref, od_ref))
    ]
    for fetch in fetches:
        fetch.start()
    pos = positions(ids_ref, ep // 16, (ep // 2) % 8, ep % 2)
    pos_col = jnp.broadcast_to(pos.astype(F32), (128, 128)).T[:, :1].astype(jnp.int32)
    mr = lax.broadcasted_iota(jnp.int32, (128, NC * RB), 1)
    hit = (mr >> 4) * CAP + (mr & 3) == pos_col
    load.wait()
    for q in range(NQ):
        take = jnp.where(hit & (((mr >> 2) & 3) == q), 1.0, 0.0).astype(BF16)
        rows = back[:, :, :QW].reshape(NC * RB, QW)
        tgrad_ref[:, q * QW : (q + 1) * QW] = jnp.dot(take, rows, preferred_element_type=F32).astype(BF16)
        if q == 0:
            gate = jnp.dot(take, back[:, :, QW:].reshape(NC * RB, 128), preferred_element_type=F32)
            ggrad_ref[...] = (gate.T[:1, :] / g_ref[...].astype(F32)).astype(BF16)
        if q < 3:
            fetches[q].wait()
            stores[q].start()
    for store in stores:
        store.wait()


def shards(tokens, cotangent, expert_ids, gates, gate_weight, up_weight, down_weight):
    rows, width = tokens.shape
    vmem, hbm = pl.BlockSpec(memory_space=pltpu.VMEM), pl.BlockSpec(memory_space=pl.ANY)
    dma = pltpu.SemaphoreType.DMA
    ids, gates = expert_ids.reshape(1, rows), gates.reshape(1, rows)
    weight_shape = jax.ShapeDtypeStruct((1, HID, width), BF16)
    back, *grads = pl.pallas_call(
        kernel,
        out_shape=(jax.ShapeDtypeStruct((NC, RB, BW), BF16),) + (weight_shape,) * 3,
        in_specs=[vmem] * 4 + [hbm] * 3,
        out_specs=(hbm,) * 4,
        scratch_shapes=[
            pltpu.VMEM((2, NC, 4 * RB, QW), BF16),
            pltpu.VMEM((2, NC, RB, QW), BF16),
            pltpu.VMEM((2, NQ * 128, QW), BF16),
            pltpu.VMEM((2, 256, 256), BF16),
            pltpu.VMEM((3, HID, width), BF16),
            pltpu.VMEM((3, width, HID), BF16),
            pltpu.VMEM((SLOTS, 4, RB, QW), BF16),
            pltpu.VMEM((2, NC, HR, QW), BF16),
            pltpu.VMEM((2, NC, RB, QW), BF16),
            pltpu.VMEM((NC, 8, 128), F32),
            pltpu.VMEM((3, NC, 8, 128), F32),
            pltpu.VMEM((NC, RB, BW), BF16),
            pltpu.VMEM((3, NC * 64, HID), BF16),
            pltpu.VMEM((3, HID, NC * 64), BF16),
            pltpu.VMEM((3, HID, width), BF16),
            dma((2, NC)), dma((2, NC)),
            dma((2, 2, NC)), dma((2, 2, NC)), dma((2, 2, NC)), dma((2, 2, NC)),
            dma((2, NC)), dma((2, NC)), dma((2, NC)), dma((2, NC)),
            dma((3, NC)), dma((3, NC)),
            dma((NC,)), dma((NC,)),
            dma((3,)), dma((3,)),
        ],
        compiler_params=pltpu.CompilerParams(
            collective_id=0, has_side_effects=True, vmem_limit_bytes=62 * 1024 * 1024
        ),
    )(
        tokens,
        cotangent,
        ids,
        gates,
        jnp.transpose(gate_weight, (0, 2, 1)),
        jnp.transpose(up_weight, (0, 2, 1)),
        down_weight,
    )
    token_grad, gates_grad, gate_grad, upper_grad, down_grad = pl.pallas_call(
        finish,
        out_shape=(
            jax.ShapeDtypeStruct((rows, width), BF16),
            jax.ShapeDtypeStruct((1, rows), BF16),
        ) + (weight_shape,) * 3,
        in_specs=[hbm, vmem, vmem] + [hbm] * 3,
        out_specs=(vmem, vmem, hbm, hbm, hbm),
        scratch_shapes=[
            pltpu.VMEM((NC, RB, BW), BF16), pltpu.VMEM((3, HID, width), BF16), dma, dma((3,)), dma((3,)),
        ],
        compiler_params=pltpu.CompilerParams(vmem_limit_bytes=62 * 1024 * 1024),
    )(back, ids, gates, *grads)
    return (
        token_grad,
        gates_grad.reshape(rows, 1),
        jnp.transpose(gate_grad, (0, 2, 1)),
        jnp.transpose(upper_grad, (0, 2, 1)),
        down_grad,
    )


def solution(mesh):
    in_specs = (
        P(("rep", "ep"), None),
        P(("rep", "ep"), None),
        P(("rep", "ep"), None),
        P(("rep", "ep"), None),
        P("ep", None, "rep"),
        P("ep", None, "rep"),
        P("ep", "rep", None),
    )
    out_specs = (
        P(("rep", "ep"), None),
        P(("rep", "ep"), None),
        P("ep", None, "rep"),
        P("ep", None, "rep"),
        P("ep", "rep", None),
    )
    return jax.shard_map(shards, mesh=mesh, in_specs=in_specs, out_specs=out_specs, check_vma=False)
```

time: 274 us -> 252 us (0.920); the launches traced: 270 us -> 252 us
  Pallas kernels: 261 us -> 251 us
  local copies, waits for them, and re-layouts: 8.02 us -> 0 us
    pallas_call x1 -> x2, Pallas kernels: 261 us -> 251 us  [the longest x1 244 us: shards(): pl.pallas_call(kernel, out_shape=(jax.ShapeDtypeStruct((NC, RB, BW), BF16...]
    unnamed x13 -> x0, local copies, waits for them, and re-layouts: 8.02 us -> none
where the time goes in v2:
time: 252 us
  Pallas kernels  251 us (100%)
    pallas_call x1, Pallas kernels, shards(): pl.pallas_call(kernel, out_shape=(jax.ShapeDtypeStruct((NC, RB, BW), BF16...  244 us
    pallas_call x1, Pallas kernels, shards(): pl.pallas_call(finish, out_shape=(jax.ShapeDtypeStruct((rows, width), BF1...  7.08 us

profile of v2, /device:TPU:97, one launch (start us, length us, event | category | flops | bytes accessed | tf_op | source)
XLA Modules:
  0.0 252.0 jit_solution(16274596179471009029)
XLA Ops:
  0.6 244.3 %shard_map.110 = (bf16[16,64,1152]{2,1,0:T(8,128)(2,1)}, bf16[1,192,4096]{2,1,0:T(8,128)(2,1)}, bf16[1,192,4096]{2,1,0:T(8,128)(2,1)}, bf16[1,192,4096]{2,1,0:T(8,128)(2,1)}) custom-call(bf16[128,4096]{1,0:T(8,128)(2,1)} %tok_ref.1, bf16[128,4096]{1,0:T(8,128)(2,1)} %cot_ref.1, s32[1,128]{1,0:T(1,128)} %bitcast.9, bf16[1,128]{1,0:T(2,128)(2,1)} %bitcast.11, ...), custom_call_target="tpu_custom_call" | custom-call | tf_op jit(solution)/shard_map/pallas_call | solution.py:384
  244.9 7.1 %shard_map.111 = (bf16[128,4096]{1,0:T(8,128)(2,1)}, bf16[1,128]{1,0:T(2,128)(2,1)}, bf16[1,192,4096]{2,1,0:T(8,128)(2,1)}, bf16[1,192,4096]{2,1,0:T(8,128)(2,1)}, bf16[1,192,4096]{2,1,0:T(8,128)(2,1)}) custom-call(bf16[16,64,1152]{2,1,0:T(8,128)(2,1)} %get-tuple-element.14.back_hbm, s32[1,128]{1,0:T(1,128)} %bitcast.10, bf16[1,128]{1,0:T(2,128)(2,1)} %bitcast.12, ...), custom_call_target="tpu_custom_call" | custom-call | tf_op jit(solution)/shard_map/pallas_call | solution.py:424

commit v3 on v2

--- a/solution.py
+++ b/solution.py
@@ -16,6 +16,9 @@
 RB = NM * NQ * CAP
 HR = RB // 2
 QW = 1024
+EW = 512
+MW = QW - EW // NQ
+MAIN = NQ * MW
 BW = QW + 128
 HID = 192
 SLOTS = 3
@@ -45,8 +48,8 @@
 def kernel(
     tok_ref, cot_ref, ids_ref, g_ref, wg_ref, wu_ref, wd_ref,
     back, dg_ref, du_ref, dd_ref,
-    land, pack, stack, perm, wnat, wtr, part, transit, full, gpart, grecv, ret, acts, acts_t, dout,
-    a2a_s, a2a_r, ag1_s, ag1_r, ag2_s, ag2_r, rs1_s, rs1_r, rs2_s, rs2_r, gt_s, gt_r, ret_s, ret_r, w_sem, o_sem,
+    land, pack, stack, eland, epack, estack, pos_own, pos_recv, perm, eperm, wnat, wtr, part, transit, full, gpart, grecv, ret, acts, acts_t, dout,
+    a2a_s, a2a_r, ea2a_s, ea2a_r, raw1_s, raw1_r, raw2_s, raw2_r, pos_s, pos_r, ag1_s, ag1_r, ag2_s, ag2_r, rs1_s, rs1_r, rs2_s, rs2_r, gt_s, gt_r, ret_s, ret_r, w_sem, o_sem,
 ):
     rep, ep = lax.axis_index("rep"), lax.axis_index("ep")
     my_y, my_z, my_c = ep // 16, (ep // 2) % 8, ep % 2
@@ -72,15 +75,22 @@
     pos = positions(ids_ref, my_y, my_z, my_c)
     gates_row = g_ref[...].astype(F32)
     gates_col = jnp.broadcast_to(gates_row, (128, 128)).T[:, :1]
+    pos_own[...] = jnp.broadcast_to(pos.astype(F32), (8, 128))
     for q in range(NQ):
-        stack[0, q * 128 : (q + 1) * 128, :] = tok_ref[:, q * QW : (q + 1) * QW]
-        cot = cot_ref[:, q * QW : (q + 1) * QW].astype(F32)
+        stack[0, q * 128 : (q + 1) * 128, :] = tok_ref[:, q * MW : (q + 1) * MW]
+        cot = cot_ref[:, q * MW : (q + 1) * MW].astype(F32)
         stack[1, q * 128 : (q + 1) * 128, :] = (cot * gates_col).astype(BF16)
+    estack[0, :128, :] = tok_ref[:, MAIN:]
+    estack[1, :128, :] = (cot_ref[:, MAIN:].astype(F32) * gates_col).astype(BF16)
 
     pr = lax.broadcasted_iota(jnp.int32, (256, 256), 0)
     pc = lax.broadcasted_iota(jnp.int32, (256, 256), 1)
     perm[0] = jnp.where(pc == ((pr & 63) >> 2) * 16 + (pr >> 6) * 4 + (pr & 3), 1.0, 0.0).astype(BF16)
     perm[1] = jnp.where(pr == ((pc & 63) >> 2) * 16 + (pc >> 6) * 4 + (pc & 3), 1.0, 0.0).astype(BF16)
+
+    er = lax.broadcasted_iota(jnp.int32, (64, 64), 0)
+    ec = lax.broadcasted_iota(jnp.int32, (64, 64), 1)
+    eperm[...] = jnp.where(ec == ((er & 15) >> 2) * 16 + (er >> 4) * 4 + (er & 3), 1.0, 0.0).astype(BF16)
 
     def partner(c, m, sign):
         z = (my_z + sign * pick(c // 2, DZ) + 8) % 8
@@ -93,57 +103,115 @@
     quarter_ok = ((sr >> 2) & 3) == (sc >> 7)
     pos4 = jnp.concatenate([pos] * NQ, axis=1)
 
+    def fill_from(source, target, places, j):
+        onehot = jnp.where(quarter_ok & (places - j * (2 * NM * CAP) == slot_of_row), 1.0, 0.0).astype(BF16)
+        for k in range(2):
+            rows = jnp.dot(onehot, source[k], preferred_element_type=F32).astype(BF16)
+            target[k, 2 * j] = rows[:RB]
+            target[k, 2 * j + 1] = rows[RB:]
+
     def fill(j, carry):
-        onehot = jnp.where(quarter_ok & (pos4 - j * (2 * NM * CAP) == slot_of_row), 1.0, 0.0).astype(BF16)
-        for k in range(2):
-            rows = jnp.dot(onehot, stack[k], preferred_element_type=F32).astype(BF16)
-            pack[k, 2 * j] = rows[:RB]
-            pack[k, 2 * j + 1] = rows[RB:]
+        fill_from(stack, pack, pos4, j)
         return carry
 
     lax.fori_loop(0, NC // 2, fill, 0)
 
-    def send(c, m):
-        rows = pl.ds(pl.multiple_of(m * 16, 16), 16)
-        for k in range(2):
-            pltpu.make_async_remote_copy(
-                src_ref=pack.at[k, c, rows],
-                dst_ref=land.at[k, c, rows],
-                send_sem=a2a_s.at[k, c],
-                recv_sem=a2a_r.at[k, c],
-                device_id=(rep, partner(c, m, 1)),
-                device_id_type=MESH,
-            ).start()
+    def send_from(source, target, send_sem, recv_sem, c):
+        def one(m, inner):
+            rows = pl.ds(pl.multiple_of(m * 16, 16), 16)
+            for k in range(2):
+                pltpu.make_async_remote_copy(
+                    src_ref=source.at[k, c, rows],
+                    dst_ref=target.at[k, c, rows],
+                    send_sem=send_sem.at[k, c],
+                    recv_sem=recv_sem.at[k, c],
+                    device_id=(rep, partner(c, m, 1)),
+                    device_id_type=MESH,
+                ).start()
+            return inner
+
+        lax.fori_loop(jnp.where(c == 0, 1, 0), NM, one, 0)
 
     def send_chunk(c, carry):
-        def one(m, inner):
-            send(c, m)
-            return inner
-
-        lax.fori_loop(jnp.where(c == 0, 1, 0), NM, one, 0)
+        send_from(pack, land, a2a_s, a2a_r, c)
         return carry
 
-    for load in loads:
-        load.wait()
-
-    def turn(j, carry):
-        cols = pl.ds(pl.multiple_of(j * 512, 512), 512)
-        for k in range(3):
-            wtr[k, cols, :] = wnat[k, :, cols].T
+    def send_extra(c, carry):
+        send_from(epack, eland, ea2a_s, ea2a_r, c)
         return carry
-
-    lax.fori_loop(0, 8, turn, 0)
-
-    pl.semaphore_wait(barrier, 66)
-    for k in range(2):
-        pltpu.make_async_copy(pack.at[k, 0, pl.ds(0, 16)], land.at[k, 0, pl.ds(0, 16)], a2a_r.at[k, 0]).start()
-    lax.fori_loop(0, 4, send_chunk, 0)
 
     def ring(src, dst, send_sem, recv_sem, peer):
         return pltpu.make_async_remote_copy(
             src_ref=src, dst_ref=dst, send_sem=send_sem, recv_sem=recv_sem,
             device_id=(peer, ep), device_id_type=MESH,
         )
+
+    def raw_one(k):
+        own = estack.at[k, pl.ds(0, 128)]
+        return (
+            ring(own, estack.at[k, pl.ds(128, 128)], raw1_s.at[k, 0], raw1_r.at[k, 0], right),
+            ring(own, estack.at[k, pl.ds(256, 128)], raw1_s.at[k, 1], raw1_r.at[k, 1], left),
+        )
+
+    def raw_two(k):
+        return (
+            ring(
+                estack.at[k, pl.ds(128, 64)], estack.at[k, pl.ds(384, 64)],
+                raw2_s.at[k, 0], raw2_r.at[k, 0], right,
+            ),
+            ring(
+                estack.at[k, pl.ds(320, 64)], estack.at[k, pl.ds(448, 64)],
+                raw2_s.at[k, 1], raw2_r.at[k, 1], left,
+            ),
+        )
+
+    pos_copies = [
+        ring(pos_own, pos_recv.at[j], pos_s.at[j], pos_r.at[j], peer) for j, peer in enumerate((right, left, across))
+    ]
+
+    pl.semaphore_wait(barrier, 66)
+    for copy in pos_copies:
+        copy.start()
+    for k in range(2):
+        for copy in raw_one(k):
+            copy.start()
+    for k in range(2):
+        pltpu.make_async_copy(pack.at[k, 0, pl.ds(0, 16)], land.at[k, 0, pl.ds(0, 16)], a2a_r.at[k, 0]).start()
+    lax.fori_loop(0, 2, send_chunk, 0)
+    for k in range(2):
+        for first, second in zip(raw_one(k), raw_two(k)):
+            first.wait_recv()
+            second.start()
+
+    def pack_extra():
+        for k in range(2):
+            for copy in raw_two(k):
+                copy.wait_recv()
+        for copy in pos_copies:
+            copy.wait_recv()
+        places = jnp.concatenate([pos_own[:1, :]] + [pos_recv[j, :1, :] for j in range(3)], axis=1).astype(jnp.int32)
+
+        def one(j, carry):
+            fill_from(estack, epack, places, j)
+            return carry
+
+        lax.fori_loop(0, NC // 2, one, 0)
+        for k in range(2):
+            pltpu.make_async_copy(
+                epack.at[k, 0, pl.ds(0, 16)], eland.at[k, 0, pl.ds(0, 16)], ea2a_r.at[k, 0]
+            ).start()
+
+    def turn_weights():
+        for load in loads:
+            load.wait()
+
+        def turn(j, carry):
+            cols = pl.ds(pl.multiple_of(j * 512, 512), 512)
+            for k in range(3):
+                wtr[k, cols, :] = wnat[k, :, cols].T
+            return carry
+
+        lax.fori_loop(0, 8, turn, 0)
 
     def gather_one(k, c):
         own = land.at[k, c, pl.ds(0, RB)]
@@ -207,13 +275,17 @@
             for copy in gather_one(k, c):
                 copy.wait_send()
         for k in range(2):
+            arrived = eland.at[k, c]
+            pltpu.make_async_copy(arrived, arrived, ea2a_r.at[k, c]).wait()
             land[k, c] = jnp.dot(perm[0], land[k, c], preferred_element_type=F32).astype(BF16)
+            eland[k, c] = jnp.dot(eperm[...], eland[k, c], preferred_element_type=F32).astype(BF16)
 
         def project(k, w):
-            return sum(
-                jnp.dot(land[k, c, q * 64 : (q + 1) * 64, :], wtr[w, q * QW : (q + 1) * QW, :], preferred_element_type=F32)
-                for q in range(NQ)
-            )
+            total = jnp.dot(eland[k, c], wtr[w, MAIN:, :], preferred_element_type=F32)
+            for q in range(NQ):
+                rows = land[k, c, q * 64 : (q + 1) * 64, :]
+                total = total + jnp.dot(rows, wtr[w, q * MW : (q + 1) * MW, :], preferred_element_type=F32)
+            return total
 
         gate_pre, up_pre, weighted = project(0, 0), project(0, 1), project(1, 2)
         logistic = jax.nn.sigmoid(gate_pre)
@@ -293,16 +365,24 @@
 
         lax.fori_loop(jnp.where(c == 0, 1, 0), NM, one, 0)
 
-    def weight_grads(j, carry):
-        q, col = j // 4, pl.ds(pl.multiple_of((j % 4) * 256, 256), 256)
-        out = pl.ds(pl.multiple_of(j * 256, 256), 256)
-        rows = pl.ds(pl.multiple_of(q * 64, 64), 64)
-        x = land[0, :, rows, col].reshape(NC * 64, 256)
-        cot = land[1, :, rows, col].reshape(NC * 64, 256)
+    def grad_tile(x, cot, at, wide):
+        out = pl.ds(pl.multiple_of(at, 128), wide)
         dout[0, :, out] = jnp.dot(acts_t[0], x, preferred_element_type=F32).astype(BF16)
         dout[1, :, out] = jnp.dot(acts_t[1], x, preferred_element_type=F32).astype(BF16)
         dout[2, :, out] = jnp.dot(acts_t[2], cot, preferred_element_type=F32).astype(BF16)
+
+    def weight_grads(q, carry):
+        rows = pl.ds(pl.multiple_of(q * 64, 64), 64)
+        for at in range(0, MW, 256):
+            wide = min(256, MW - at)
+            x, cot = (land[k, :, rows, at : at + wide].reshape(NC * 64, wide) for k in range(2))
+            grad_tile(x, cot, q * MW + at, wide)
         return carry
+
+    def weight_grads_extra():
+        for at in range(0, EW, 256):
+            x, cot = (eland[k, :, :, at : at + 256].reshape(NC * 64, 256) for k in range(2))
+            grad_tile(x, cot, MAIN + at, 256)
 
     def turn_acts():
         for k in range(3):
@@ -311,14 +391,20 @@
     def step(t, carry):
         pl.when(t < NC)(lambda: step_gather_one(t))
         pl.when((t >= 1) & (t < NC + 1))(lambda: step_gather_two(t - 1))
-        lax.fori_loop(jnp.where(t < 2, 4 + 6 * t, NC), jnp.where(t < 2, 10 + 6 * t, NC), send_chunk, 0)
+        pl.when(t == 1)(pack_extra)
+        main_first, main_last = pick(t, (2, 6, 9, 12)), pick(t, (6, 9, 12, 16))
+        extra_first, extra_last = pick(t, (0, 0, 4, 9)), pick(t, (0, 4, 9, 16))
+        lax.fori_loop(extra_first, extra_last, send_extra, 0)
+        lax.fori_loop(main_first, main_last, send_chunk, 0)
+        pl.when(t == 1)(turn_weights)
         pl.when((t >= 2) & (t < NC + 2))(lambda: step_compute(t - 2))
         pl.when((t >= 3) & (t < NC + 3))(lambda: step_scatter_two(t - 3))
         pl.when((t >= 4) & (t < NC + 4))(lambda: step_return(t - 4))
         pl.when(t == NC + 1)(turn_acts)
-        first = jnp.where(t == NC + 1, 0, jnp.where(t == NC + 2, 4, 10))
-        last = jnp.where(t == NC + 1, 4, jnp.where(t == NC + 2, 10, jnp.where(t == NC + 3, 16, 0)))
+        first = jnp.where(t == NC + 1, 0, jnp.where(t == NC + 2, 1, 3))
+        last = jnp.where(t == NC + 1, 1, jnp.where(t == NC + 2, 3, jnp.where(t == NC + 3, 4, 0)))
         lax.fori_loop(first, last, weight_grads, 0)
+        pl.when(t == NC + 3)(weight_grads_extra)
         return carry
 
     lax.fori_loop(0, NC + 4, step, 0)
@@ -335,7 +421,13 @@
         rows = skip if c == 0 else pl.ds(0, RB)
         for k in range(2):
             pltpu.make_async_copy(pack.at[k, c, rows], pack.at[k, c, rows], a2a_s.at[k, c]).wait()
+            pltpu.make_async_copy(epack.at[k, c, rows], epack.at[k, c, rows], ea2a_s.at[k, c]).wait()
         pltpu.make_async_copy(ret.at[c, rows], ret.at[c, rows], ret_s.at[c]).wait()
+    for k in range(2):
+        for copy in raw_one(k) + raw_two(k):
+            copy.wait_send()
+    for copy in pos_copies:
+        copy.wait_send()
     for store in stores:
         store.wait()
 
@@ -387,10 +479,16 @@
         in_specs=[vmem] * 4 + [hbm] * 3,
         out_specs=(hbm,) * 4,
         scratch_shapes=[
-            pltpu.VMEM((2, NC, 4 * RB, QW), BF16),
-            pltpu.VMEM((2, NC, RB, QW), BF16),
-            pltpu.VMEM((2, NQ * 128, QW), BF16),
+            pltpu.VMEM((2, NC, 4 * RB, MW), BF16),
+            pltpu.VMEM((2, NC, RB, MW), BF16),
+            pltpu.VMEM((2, NQ * 128, MW), BF16),
+            pltpu.VMEM((2, NC, RB, EW), BF16),
+            pltpu.VMEM((2, NC, RB, EW), BF16),
+            pltpu.VMEM((2, 4 * 128, EW), BF16),
+            pltpu.VMEM((8, 128), F32),
+            pltpu.VMEM((3, 8, 128), F32),
             pltpu.VMEM((2, 256, 256), BF16),
+            pltpu.VMEM((64, 64), BF16),
             pltpu.VMEM((3, HID, width), BF16),
             pltpu.VMEM((3, width, HID), BF16),
             pltpu.VMEM((SLOTS, 4, RB, QW), BF16),
@@ -402,7 +500,8 @@
             pltpu.VMEM((3, NC * 64, HID), BF16),
             pltpu.VMEM((3, HID, NC * 64), BF16),
             pltpu.VMEM((3, HID, width), BF16),
-            dma((2, NC)), dma((2, NC)),
+            dma((2, NC)), dma((2, NC)), dma((2, NC)), dma((2, NC)),
+            dma((2, 2)), dma((2, 2)), dma((2, 2)), dma((2, 2)), dma((3,)), dma((3,)),
             dma((2, 2, NC)), dma((2, 2, NC)), dma((2, 2, NC)), dma((2, 2, NC)),
             dma((2, NC)), dma((2, NC)), dma((2, NC)), dma((2, NC)),
             dma((3, NC)), dma((3, NC)),

time: 252 us -> 236 us (0.937); the launches traced: 252 us -> 233 us
  Pallas kernels: 251 us -> 232 us
    pallas_call x1, Pallas kernels: 244 us -> 225 us  [shards(): pl.pallas_call(kernel, out_shape=(jax.ShapeDtypeStruct((NC, RB, BW), BF16...]
where the time goes in v3:
time: 236 us; the launch traced here: 233 us
  Pallas kernels  232 us (98%)
    pallas_call x1, Pallas kernels, shards(): pl.pallas_call(kernel, out_shape=(jax.ShapeDtypeStruct((NC, RB, BW), BF16...  225 us
    pallas_call x1, Pallas kernels, shards(): pl.pallas_call(finish, out_shape=(jax.ShapeDtypeStruct((rows, width), BF1...  7.08 us

profile of v3, /device:TPU:97, one launch (start us, length us, event | category | flops | bytes accessed | tf_op | source)
XLA Modules:
  0.0 232.5 jit_solution(7860308044522341702)
XLA Ops:
  0.6 224.8 %shard_map.110 = (bf16[16,64,1152]{2,1,0:T(8,128)(2,1)}, bf16[1,192,4096]{2,1,0:T(8,128)(2,1)}, bf16[1,192,4096]{2,1,0:T(8,128)(2,1)}, bf16[1,192,4096]{2,1,0:T(8,128)(2,1)}) custom-call(bf16[128,4096]{1,0:T(8,128)(2,1)} %tok_ref.1, bf16[128,4096]{1,0:T(8,128)(2,1)} %cot_ref.1, s32[1,128]{1,0:T(1,128)} %bitcast.9, bf16[1,128]{1,0:T(2,128)(2,1)} %bitcast.11, ...), custom_call_target="tpu_custom_call" | custom-call | tf_op jit(solution)/shard_map/pallas_call | solution.py:476
  225.5 7.1 %shard_map.111 = (bf16[128,4096]{1,0:T(8,128)(2,1)}, bf16[1,128]{1,0:T(2,128)(2,1)}, bf16[1,192,4096]{2,1,0:T(8,128)(2,1)}, bf16[1,192,4096]{2,1,0:T(8,128)(2,1)}, bf16[1,192,4096]{2,1,0:T(8,128)(2,1)}) custom-call(bf16[16,64,1152]{2,1,0:T(8,128)(2,1)} %get-tuple-element.14.back_hbm, s32[1,128]{1,0:T(1,128)} %bitcast.10, bf16[1,128]{1,0:T(2,128)(2,1)} %bitcast.12, ...), custom_call_target="tpu_custom_call" | custom-call | tf_op jit(solution)/shard_map/pallas_call | solution.py:523

commit v4 on v3

--- a/solution.py
+++ b/solution.py
@@ -8,7 +8,7 @@
 MESH = pl.DeviceIdType.MESH
 F32, BF16 = jnp.float32, jnp.bfloat16
 
-DZ = (0, 7, 2, 5, 4, 3, 6, 1)
+DZ = (0, 7, 2, 5, 3, 4, 6, 1)
 NC = 16
 NM = 4
 CAP = 4
@@ -16,6 +16,7 @@
 RB = NM * NQ * CAP
 HR = RB // 2
 QW = 1024
+HW = 512
 EW = 512
 MW = QW - EW // NQ
 MAIN = NQ * MW
@@ -48,12 +49,15 @@
 def kernel(
     tok_ref, cot_ref, ids_ref, g_ref, wg_ref, wu_ref, wd_ref,
     back, dg_ref, du_ref, dd_ref,
-    land, pack, stack, eland, epack, estack, pos_own, pos_recv, perm, eperm, wnat, wtr, part, transit, full, gpart, grecv, ret, acts, acts_t, dout,
-    a2a_s, a2a_r, ea2a_s, ea2a_r, raw1_s, raw1_r, raw2_s, raw2_r, pos_s, pos_r, ag1_s, ag1_r, ag2_s, ag2_r, rs1_s, rs1_r, rs2_s, rs2_r, gt_s, gt_r, ret_s, ret_r, w_sem, o_sem,
+    land, pack, stack, eland, epack, estack, pos_own, pos_recv, perm, eperm, wnat, wtr, wpair, pre_own, pre_pair, part, first, second, gpart, grecv, ret, acts, acts_t, dout,
+    a2a_s, a2a_r, ea2a_s, ea2a_r, raw1_s, raw1_r, raw2_s, raw2_r, pos_s, pos_r, ag1_s, ag1_r, ag2_s, ag2_r, rs1_s, rs1_r, rs2_s, rs2_r, pre_s, pre_r, wx_s, wx_r, gt_s, gt_r, ret_s, ret_r, w_sem, o_sem,
 ):
     rep, ep = lax.axis_index("rep"), lax.axis_index("ep")
     my_y, my_z, my_c = ep // 16, (ep // 2) % 8, ep % 2
-    right, left, across = (rep + 1) % 4, (rep + 3) % 4, (rep + 2) % 4
+    side = 1 - 2 * ((rep + my_c) % 2)
+    pair, other, across = (rep + side + 4) % 4, (rep - side + 4) % 4, (rep + 2) % 4
+    half = ((rep + 1 - my_c) // 2) % 2
+    mine, theirs = (pl.ds(pl.multiple_of(h * 2048, 2048), 2048) for h in (half, 1 - half))
 
     loads = [
         pltpu.make_async_copy(src.at[0], wnat.at[k], w_sem.at[k])
@@ -69,7 +73,7 @@
         return carry
 
     lax.fori_loop(1, 64, greet, 0)
-    for peer in (left, right, across):
+    for peer in (pair, other, across):
         pl.semaphore_signal(barrier, inc=1, device_id=(peer, ep), device_id_type=MESH)
 
     pos = positions(ids_ref, my_y, my_z, my_c)
@@ -100,18 +104,21 @@
     sr = lax.broadcasted_iota(jnp.int32, (2 * RB, 512), 0)
     sc = lax.broadcasted_iota(jnp.int32, (2 * RB, 512), 1)
     slot_of_row = (sr >> 4) * CAP + (sr & 3)
-    quarter_ok = ((sr >> 2) & 3) == (sc >> 7)
+    quarter = (sr >> 2) & 3
+    quarter_ok = quarter == (sc >> 7)
+    changed = (sr >= RB) & ((quarter == 1) | (quarter == 2))
+    block_ok = jnp.where(changed, 3 - quarter, quarter) == (sc >> 7)
     pos4 = jnp.concatenate([pos] * NQ, axis=1)
 
-    def fill_from(source, target, places, j):
-        onehot = jnp.where(quarter_ok & (places - j * (2 * NM * CAP) == slot_of_row), 1.0, 0.0).astype(BF16)
+    def fill_from(source, target, ok, places, j):
+        onehot = jnp.where(ok & (places - j * (2 * NM * CAP) == slot_of_row), 1.0, 0.0).astype(BF16)
         for k in range(2):
             rows = jnp.dot(onehot, source[k], preferred_element_type=F32).astype(BF16)
             target[k, 2 * j] = rows[:RB]
             target[k, 2 * j + 1] = rows[RB:]
 
     def fill(j, carry):
-        fill_from(stack, pack, pos4, j)
+        fill_from(stack, pack, quarter_ok, pos4, j)
         return carry
 
     lax.fori_loop(0, NC // 2, fill, 0)
@@ -149,24 +156,27 @@
     def raw_one(k):
         own = estack.at[k, pl.ds(0, 128)]
         return (
-            ring(own, estack.at[k, pl.ds(128, 128)], raw1_s.at[k, 0], raw1_r.at[k, 0], right),
-            ring(own, estack.at[k, pl.ds(256, 128)], raw1_s.at[k, 1], raw1_r.at[k, 1], left),
+            ring(own, estack.at[k, pl.ds(128, 128)], raw1_s.at[k, 0], raw1_r.at[k, 0], pair),
+            ring(own, estack.at[k, pl.ds(256, 128)], raw1_s.at[k, 1], raw1_r.at[k, 1], other),
         )
 
     def raw_two(k):
         return (
             ring(
                 estack.at[k, pl.ds(128, 64)], estack.at[k, pl.ds(384, 64)],
-                raw2_s.at[k, 0], raw2_r.at[k, 0], right,
+                raw2_s.at[k, 0], raw2_r.at[k, 0], other,
             ),
             ring(
                 estack.at[k, pl.ds(320, 64)], estack.at[k, pl.ds(448, 64)],
-                raw2_s.at[k, 1], raw2_r.at[k, 1], left,
+                raw2_s.at[k, 1], raw2_r.at[k, 1], pair,
             ),
         )
 
     pos_copies = [
-        ring(pos_own, pos_recv.at[j], pos_s.at[j], pos_r.at[j], peer) for j, peer in enumerate((right, left, across))
+        ring(pos_own, pos_recv.at[j], pos_s.at[j], pos_r.at[j], peer) for j, peer in enumerate((pair, other, across))
+    ]
+    weight_copies = [
+        ring(wnat.at[k, :, theirs], wpair.at[pl.ds(k * HID, HID)], wx_s.at[k], wx_r.at[k], pair) for k in range(2)
     ]
 
     pl.semaphore_wait(barrier, 66)
@@ -179,9 +189,11 @@
         pltpu.make_async_copy(pack.at[k, 0, pl.ds(0, 16)], land.at[k, 0, pl.ds(0, 16)], a2a_r.at[k, 0]).start()
     lax.fori_loop(0, 2, send_chunk, 0)
     for k in range(2):
-        for first, second in zip(raw_one(k), raw_two(k)):
-            first.wait_recv()
-            second.start()
+        for one, two in zip(raw_one(k), raw_two(k)):
+            one.wait_recv()
+            two.start()
+    for load in loads:
+        load.wait()
 
     def pack_extra():
         for k in range(2):
@@ -192,7 +204,7 @@
         places = jnp.concatenate([pos_own[:1, :]] + [pos_recv[j, :1, :] for j in range(3)], axis=1).astype(jnp.int32)
 
         def one(j, carry):
-            fill_from(estack, epack, places, j)
+            fill_from(estack, epack, block_ok, places, j)
             return carry
 
         lax.fori_loop(0, NC // 2, one, 0)
@@ -202,9 +214,6 @@
             ).start()
 
     def turn_weights():
-        for load in loads:
-            load.wait()
-
         def turn(j, carry):
             cols = pl.ds(pl.multiple_of(j * 512, 512), 512)
             for k in range(3):
@@ -216,40 +225,35 @@
     def gather_one(k, c):
         own = land.at[k, c, pl.ds(0, RB)]
         return (
-            ring(own, land.at[k, c, pl.ds(RB, RB)], ag1_s.at[k, 0, c], ag1_r.at[k, 0, c], right),
-            ring(own, land.at[k, c, pl.ds(2 * RB, RB)], ag1_s.at[k, 1, c], ag1_r.at[k, 1, c], left),
+            ring(own, land.at[k, c, pl.ds(RB, RB)], ag1_s.at[k, 0, c], ag1_r.at[k, 0, c], pair),
+            ring(own, land.at[k, c, pl.ds(2 * RB, RB)], ag1_s.at[k, 1, c], ag1_r.at[k, 1, c], other),
         )
 
     def gather_two(k, c):
         return (
             ring(
                 land.at[k, c, pl.ds(RB, HR)], land.at[k, c, pl.ds(3 * RB, HR)],
-                ag2_s.at[k, 0, c], ag2_r.at[k, 0, c], right,
+                ag2_s.at[k, 0, c], ag2_r.at[k, 0, c], other,
             ),
             ring(
                 land.at[k, c, pl.ds(2 * RB + HR, HR)], land.at[k, c, pl.ds(3 * RB + HR, HR)],
-                ag2_s.at[k, 1, c], ag2_r.at[k, 1, c], left,
+                ag2_s.at[k, 1, c], ag2_r.at[k, 1, c], pair,
             ),
         )
 
+    def pre_copy(c):
+        return ring(pre_own.at[c], pre_pair.at[c], pre_s.at[c], pre_r.at[c], pair)
+
     def scatter_one(c):
-        p = c % SLOTS
-        return (
-            ring(part.at[p, 3, pl.ds(0, HR)], transit.at[0, c], rs1_s.at[0, c], rs1_r.at[0, c], right),
-            ring(part.at[p, 3, pl.ds(HR, HR)], transit.at[1, c], rs1_s.at[1, c], rs1_r.at[1, c], left),
-        )
+        return ring(part.at[c % SLOTS, pl.ds(2 * RB, 2 * RB)], first.at[c], rs1_s.at[c], rs1_r.at[c], other)
 
     def scatter_two(c):
-        p = c % SLOTS
-        return (
-            ring(part.at[p, 2], full.at[0, c], rs2_s.at[0, c], rs2_r.at[0, c], right),
-            ring(part.at[p, 1], full.at[1, c], rs2_s.at[1, c], rs2_r.at[1, c], left),
-        )
+        return ring(part.at[c % SLOTS, pl.ds(RB, RB)], second.at[c], rs2_s.at[c], rs2_r.at[c], pair)
 
     def gate_copies(c):
         return [
             ring(gpart.at[c], grecv.at[j, c], gt_s.at[j, c], gt_r.at[j, c], peer)
-            for j, peer in enumerate((right, left, across))
+            for j, peer in enumerate((pair, other, across))
         ]
 
     def step_gather_one(c):
@@ -261,13 +265,11 @@
 
     def step_gather_two(c):
         for k in range(2):
-            firsts, seconds = gather_one(k, c), gather_two(k, c)
-            for first, second in zip(firsts, seconds):
-                first.wait_recv()
-                second.start()
+            for one, two in zip(gather_one(k, c), gather_two(k, c)):
+                one.wait_recv()
+                two.start()
 
     def step_compute(c):
-        p = c % SLOTS
         for k in range(2):
             for copy in gather_two(k, c):
                 copy.wait_recv()
@@ -295,32 +297,35 @@
         up_grad = (weighted * activated).astype(BF16)
         gate_sum = jnp.sum(hidden.astype(F32) * weighted, axis=1, keepdims=True)
         gate_sum = jnp.broadcast_to(jnp.concatenate([gate_sum, gate_sum], axis=0), (128, 128))
-        gpart[c] = gate_sum.T[:8, :]
+        gpart[c] = gate_sum.T[:1, :]
         rows = pl.ds(pl.multiple_of(c * 64, 64), 64)
         acts[0, rows, :] = pre_grad
         acts[1, rows, :] = up_grad
         acts[2, rows, :] = hidden
+        pre_own[c] = jnp.concatenate([pre_grad, up_grad], axis=1)
+        pre_copy(c).start()
         for copy in gate_copies(c):
             copy.start()
-        parts = []
-        for q in range(NQ):
-            both = jnp.dot(pre_grad, wnat[0, :, q * QW : (q + 1) * QW], preferred_element_type=F32)
-            both = both + jnp.dot(up_grad, wnat[1, :, q * QW : (q + 1) * QW], preferred_element_type=F32)
-            parts.append(both.astype(BF16))
-        message = jnp.dot(perm[1], jnp.concatenate(parts, axis=0), preferred_element_type=F32).astype(BF16)
-        for rel in range(4):
-            part[p, rel] = message[rel * RB : (rel + 1) * RB]
-        for copy in scatter_one(c):
-            copy.start()
+
+    def step_scatter_one(c):
+        rows = pl.ds(pl.multiple_of(c * 64, 64), 64)
+        total = jnp.dot(acts[0, rows, :], wnat[0, :, mine], preferred_element_type=F32)
+        total = total + jnp.dot(acts[1, rows, :], wnat[1, :, mine], preferred_element_type=F32)
+        pl.when(c == 0)(lambda: [copy.wait_recv() for copy in weight_copies] and None)
+        pre_copy(c).wait()
+        swapped = jnp.concatenate([pre_pair[c, b * 16 : (b + 1) * 16, :] for b in (1, 0, 3, 2)], axis=0)
+        total = total + jnp.dot(swapped, wpair[...], preferred_element_type=F32)
+        total = total.astype(BF16)
+        stacked = jnp.concatenate([total[:, q * HW : (q + 1) * HW] for q in range(NQ)], axis=0)
+        part[c % SLOTS] = jnp.dot(perm[1], stacked, preferred_element_type=F32).astype(BF16)
+        scatter_one(c).start()
 
     def step_scatter_two(c):
         p = c % SLOTS
-        ones, twos = scatter_one(c), scatter_two(c)
-        for j, (rel, rows) in enumerate(((2, pl.ds(0, HR)), (1, pl.ds(HR, HR)))):
-            ones[j].wait_recv()
-            total = part[p, rel, rows, :].astype(F32) + transit[j, c].astype(F32)
-            part[p, rel, rows, :] = total.astype(BF16)
-            twos[j].start()
+        scatter_one(c).wait_recv()
+        total = part[p, RB : 2 * RB, :].astype(F32) + first[c, RB:, :].astype(F32)
+        part[p, RB : 2 * RB, :] = total.astype(BF16)
+        scatter_two(c).start()
 
     gr = lax.broadcasted_iota(jnp.int32, (RB, 128), 0)
     gl = lax.broadcasted_iota(jnp.int32, (RB, 128), 1)
@@ -339,19 +344,17 @@
 
     def step_return(c):
         p = c % SLOTS
-        for copy in scatter_two(c):
-            copy.wait_recv()
-            copy.wait_send()
-        for copy in scatter_one(c):
-            copy.wait_send()
+        scatter_two(c).wait()
+        scatter_one(c).wait_send()
         for copy in gate_copies(c):
             copy.wait()
-        total = part[p, 0].astype(F32) + full[0, c].astype(F32) + full[1, c].astype(F32)
-        ret[c, :, :QW] = total.astype(BF16)
-        gate = jnp.where(gl == slot_lane, gpart[c, :1, :], 0.0)
-        gate = gate + jnp.where(gl == slot_lane + 2 * NM * CAP, grecv[0, c, :1, :], 0.0)
-        gate = gate + jnp.where(gl == slot_lane + NM * CAP, grecv[1, c, :1, :], 0.0)
-        gate = gate + jnp.where(gl == slot_lane + 3 * NM * CAP, grecv[2, c, :1, :], 0.0)
+        total = part[p, :RB, :].astype(F32) + first[c, :RB, :].astype(F32)
+        ret[c, :, pl.ds(pl.multiple_of(half * HW, HW), HW)] = total.astype(BF16)
+        ret[c, :, pl.ds(pl.multiple_of((1 - half) * HW, HW), HW)] = second[c]
+        gate = jnp.where(gl == slot_lane, gpart[c], 0.0)
+        gate = gate + jnp.where(gl == slot_lane + NM * CAP, grecv[0, c], 0.0)
+        gate = gate + jnp.where(gl == slot_lane + 2 * NM * CAP, grecv[1, c], 0.0)
+        gate = gate + jnp.where(gl == slot_lane + 3 * NM * CAP, grecv[2, c], 0.0)
         gate = jnp.sum(gate, axis=1, keepdims=True)
         ret[c, :, QW:] = jnp.broadcast_to(gate, (RB, 128)).astype(BF16)
 
@@ -397,17 +400,18 @@
         lax.fori_loop(extra_first, extra_last, send_extra, 0)
         lax.fori_loop(main_first, main_last, send_chunk, 0)
         pl.when(t == 1)(turn_weights)
+        pl.when(t == 1)(lambda: [copy.start() for copy in weight_copies] and None)
         pl.when((t >= 2) & (t < NC + 2))(lambda: step_compute(t - 2))
-        pl.when((t >= 3) & (t < NC + 3))(lambda: step_scatter_two(t - 3))
-        pl.when((t >= 4) & (t < NC + 4))(lambda: step_return(t - 4))
+        pl.when((t >= 3) & (t < NC + 3))(lambda: step_scatter_one(t - 3))
+        pl.when((t >= 4) & (t < NC + 4))(lambda: step_scatter_two(t - 4))
+        pl.when((t >= 5) & (t < NC + 5))(lambda: step_return(t - 5))
         pl.when(t == NC + 1)(turn_acts)
-        first = jnp.where(t == NC + 1, 0, jnp.where(t == NC + 2, 1, 3))
-        last = jnp.where(t == NC + 1, 1, jnp.where(t == NC + 2, 3, jnp.where(t == NC + 3, 4, 0)))
-        lax.fori_loop(first, last, weight_grads, 0)
-        pl.when(t == NC + 3)(weight_grads_extra)
+        u = t - NC
+        lax.fori_loop(pick(u, (0, 0, 1, 2)), pick(u, (0, 1, 2, 4)), weight_grads, 0)
+        pl.when(t == NC + 4)(weight_grads_extra)
         return carry
 
-    lax.fori_loop(0, NC + 4, step, 0)
+    lax.fori_loop(0, NC + 5, step, 0)
 
     stores = [
         pltpu.make_async_copy(dout.at[k], dst.at[0], o_sem.at[k])
@@ -426,7 +430,7 @@
     for k in range(2):
         for copy in raw_one(k) + raw_two(k):
             copy.wait_send()
-    for copy in pos_copies:
+    for copy in pos_copies + weight_copies:
         copy.wait_send()
     for store in stores:
         store.wait()
@@ -456,7 +460,10 @@
     for q in range(NQ):
         take = jnp.where(hit & (((mr >> 2) & 3) == q), 1.0, 0.0).astype(BF16)
         rows = back[:, :, :QW].reshape(NC * RB, QW)
-        tgrad_ref[:, q * QW : (q + 1) * QW] = jnp.dot(take, rows, preferred_element_type=F32).astype(BF16)
+        found = jnp.dot(take, rows, preferred_element_type=F32).astype(BF16)
+        for h in range(2):
+            at = h * 2048 + q * HW
+            tgrad_ref[:, at : at + HW] = found[:, h * HW : (h + 1) * HW]
         if q == 0:
             gate = jnp.dot(take, back[:, :, QW:].reshape(NC * RB, 128), preferred_element_type=F32)
             ggrad_ref[...] = (gate.T[:1, :] / g_ref[...].astype(F32)).astype(BF16)
@@ -491,11 +498,14 @@
             pltpu.VMEM((64, 64), BF16),
             pltpu.VMEM((3, HID, width), BF16),
             pltpu.VMEM((3, width, HID), BF16),
-            pltpu.VMEM((SLOTS, 4, RB, QW), BF16),
-            pltpu.VMEM((2, NC, HR, QW), BF16),
-            pltpu.VMEM((2, NC, RB, QW), BF16),
-            pltpu.VMEM((NC, 8, 128), F32),
-            pltpu.VMEM((3, NC, 8, 128), F32),
+            pltpu.VMEM((2 * HID, width // 2), BF16),
+            pltpu.VMEM((NC, 64, 2 * HID), BF16),
+            pltpu.VMEM((NC, 64, 2 * HID), BF16),
+            pltpu.VMEM((SLOTS, 4 * RB, HW), BF16),
+            pltpu.VMEM((NC, 2 * RB, HW), BF16),
+            pltpu.VMEM((NC, RB, HW), BF16),
+            pltpu.VMEM((NC, 1, 128), F32),
+            pltpu.VMEM((3, NC, 1, 128), F32),
             pltpu.VMEM((NC, RB, BW), BF16),
             pltpu.VMEM((3, NC * 64, HID), BF16),
             pltpu.VMEM((3, HID, NC * 64), BF16),
@@ -503,7 +513,7 @@
             dma((2, NC)), dma((2, NC)), dma((2, NC)), dma((2, NC)),
             dma((2, 2)), dma((2, 2)), dma((2, 2)), dma((2, 2)), dma((3,)), dma((3,)),
             dma((2, 2, NC)), dma((2, 2, NC)), dma((2, 2, NC)), dma((2, 2, NC)),
-            dma((2, NC)), dma((2, NC)), dma((2, NC)), dma((2, NC)),
+            dma((NC,)), dma((NC,)), dma((NC,)), dma((NC,)), dma((NC,)), dma((NC,)), dma((2,)), dma((2,)),
             dma((3, NC)), dma((3, NC)),
             dma((NC,)), dma((NC,)),
             dma((3,)), dma((3,)),

time: 236 us -> 231 us (0.979)
  Pallas kernels: 232 us -> 228 us
    pallas_call x1, Pallas kernels: 225 us -> 220 us  [shards(): pl.pallas_call(kernel, out_shape=(jax.ShapeDtypeStruct((NC, RB, BW), BF16...]
where the time goes in v4:
time: 231 us; the launch traced here: 228 us
  Pallas kernels  228 us (99%)
    pallas_call x1, Pallas kernels, shards(): pl.pallas_call(kernel, out_shape=(jax.ShapeDtypeStruct((NC, RB, BW), BF16...  220 us
    pallas_call x1, Pallas kernels, shards(): pl.pallas_call(finish, out_shape=(jax.ShapeDtypeStruct((rows, width), BF1...  7.08 us

profile of v4, /device:TPU:97, one launch (start us, length us, event | category | flops | bytes accessed | tf_op | source)
XLA Modules:
  0.0 228.2 jit_solution(1729817798185552933)
XLA Ops:
  0.6 220.5 %shard_map.110 = (bf16[16,64,1152]{2,1,0:T(8,128)(2,1)}, bf16[1,192,4096]{2,1,0:T(8,128)(2,1)}, bf16[1,192,4096]{2,1,0:T(8,128)(2,1)}, bf16[1,192,4096]{2,1,0:T(8,128)(2,1)}) custom-call(bf16[128,4096]{1,0:T(8,128)(2,1)} %tok_ref.1, bf16[128,4096]{1,0:T(8,128)(2,1)} %cot_ref.1, s32[1,128]{1,0:T(1,128)} %bitcast.9, bf16[1,128]{1,0:T(2,128)(2,1)} %bitcast.11, ...), custom_call_target="tpu_custom_call" | custom-call | tf_op jit(solution)/shard_map/pallas_call | solution.py:483
  221.1 7.1 %shard_map.111 = (bf16[128,4096]{1,0:T(8,128)(2,1)}, bf16[1,128]{1,0:T(2,128)(2,1)}, bf16[1,192,4096]{2,1,0:T(8,128)(2,1)}, bf16[1,192,4096]{2,1,0:T(8,128)(2,1)}, bf16[1,192,4096]{2,1,0:T(8,128)(2,1)}) custom-call(bf16[16,64,1152]{2,1,0:T(8,128)(2,1)} %get-tuple-element.14.back_hbm, s32[1,128]{1,0:T(1,128)} %bitcast.10, bf16[1,128]{1,0:T(2,128)(2,1)} %bitcast.12, ...), custom_call_target="tpu_custom_call" | custom-call | tf_op jit(solution)/shard_map/pallas_call | solution.py:533

commit v5 on v4

--- a/solution.py
+++ b/solution.py
@@ -407,7 +407,7 @@
         pl.when((t >= 5) & (t < NC + 5))(lambda: step_return(t - 5))
         pl.when(t == NC + 1)(turn_acts)
         u = t - NC
-        lax.fori_loop(pick(u, (0, 0, 1, 2)), pick(u, (0, 1, 2, 4)), weight_grads, 0)
+        lax.fori_loop(pick(u, (0, 0, 1, 2, 3)), pick(u, (0, 1, 2, 3, 4)), weight_grads, 0)
         pl.when(t == NC + 4)(weight_grads_extra)
         return carry
 
@@ -457,6 +457,9 @@
     mr = lax.broadcasted_iota(jnp.int32, (128, NC * RB), 1)
     hit = (mr >> 4) * CAP + (mr & 3) == pos_col
     load.wait()
+    for fetch, store in zip(fetches, stores):
+        fetch.wait()
+        store.start()
     for q in range(NQ):
         take = jnp.where(hit & (((mr >> 2) & 3) == q), 1.0, 0.0).astype(BF16)
         rows = back[:, :, :QW].reshape(NC * RB, QW)
@@ -467,9 +470,6 @@
         if q == 0:
             gate = jnp.dot(take, back[:, :, QW:].reshape(NC * RB, 128), preferred_element_type=F32)
             ggrad_ref[...] = (gate.T[:1, :] / g_ref[...].astype(F32)).astype(BF16)
-        if q < 3:
-            fetches[q].wait()
-            stores[q].start()
     for store in stores:
         store.wait()
 

time: 231 us -> 229 us (level)
  no operation moved by 1% of the time
where the time goes in v5:
time: 229 us; the launch traced here: 227 us
  Pallas kernels  227 us (99%)
    pallas_call x1, Pallas kernels, shards(): pl.pallas_call(kernel, out_shape=(jax.ShapeDtypeStruct((NC, RB, BW), BF16...  220 us
    pallas_call x1, Pallas kernels, shards(): pl.pallas_call(finish, out_shape=(jax.ShapeDtypeStruct((rows, width), BF1...  6.52 us

profile of v5, /device:TPU:97, one launch (start us, length us, event | category | flops | bytes accessed | tf_op | source)
XLA Modules:
  0.0 227.4 jit_solution(7453584998544167502)
XLA Ops:
  0.6 220.3 %shard_map.110 = (bf16[16,64,1152]{2,1,0:T(8,128)(2,1)}, bf16[1,192,4096]{2,1,0:T(8,128)(2,1)}, bf16[1,192,4096]{2,1,0:T(8,128)(2,1)}, bf16[1,192,4096]{2,1,0:T(8,128)(2,1)}) custom-call(bf16[128,4096]{1,0:T(8,128)(2,1)} %tok_ref.1, bf16[128,4096]{1,0:T(8,128)(2,1)} %cot_ref.1, s32[1,128]{1,0:T(1,128)} %bitcast.9, bf16[1,128]{1,0:T(2,128)(2,1)} %bitcast.11, ...), custom_call_target="tpu_custom_call" | custom-call | tf_op jit(solution)/shard_map/pallas_call | solution.py:483
  220.9 6.5 %shard_map.111 = (bf16[128,4096]{1,0:T(8,128)(2,1)}, bf16[1,128]{1,0:T(2,128)(2,1)}, bf16[1,192,4096]{2,1,0:T(8,128)(2,1)}, bf16[1,192,4096]{2,1,0:T(8,128)(2,1)}, bf16[1,192,4096]{2,1,0:T(8,128)(2,1)}) custom-call(bf16[16,64,1152]{2,1,0:T(8,128)(2,1)} %get-tuple-element.14.back_hbm, s32[1,128]{1,0:T(1,128)} %bitcast.10, bf16[1,128]{1,0:T(2,128)(2,1)} %bitcast.12, ...), custom_call_target="tpu_custom_call" | custom-call | tf_op jit(solution)/shard_map/pallas_call | solution.py:533

commit v6 on v5

--- a/solution.py
+++ b/solution.py
@@ -121,7 +121,7 @@
         fill_from(stack, pack, quarter_ok, pos4, j)
         return carry
 
-    lax.fori_loop(0, NC // 2, fill, 0)
+    fill(0, 0)
 
     def send_from(source, target, send_sem, recv_sem, c):
         def one(m, inner):
@@ -188,6 +188,7 @@
     for k in range(2):
         pltpu.make_async_copy(pack.at[k, 0, pl.ds(0, 16)], land.at[k, 0, pl.ds(0, 16)], a2a_r.at[k, 0]).start()
     lax.fori_loop(0, 2, send_chunk, 0)
+    lax.fori_loop(1, NC // 2, fill, 0)
     for k in range(2):
         for one, two in zip(raw_one(k), raw_two(k)):
             one.wait_recv()

time: 229 us -> 229 us (level)
  no operation moved by 1% of the time
where the time goes in v6:
time: 229 us; the launch traced here: 227 us
  Pallas kernels  226 us (99%)
    pallas_call x1, Pallas kernels, shards(): pl.pallas_call(kernel, out_shape=(jax.ShapeDtypeStruct((NC, RB, BW), BF16...  220 us
    pallas_call x1, Pallas kernels, shards(): pl.pallas_call(finish, out_shape=(jax.ShapeDtypeStruct((rows, width), BF1...  6.52 us

profile of v6, /device:TPU:97, one launch (start us, length us, event | category | flops | bytes accessed | tf_op | source)
XLA Modules:
  0.0 226.9 jit_solution(13061211287821840395)
XLA Ops:
  0.6 219.7 %shard_map.110 = (bf16[16,64,1152]{2,1,0:T(8,128)(2,1)}, bf16[1,192,4096]{2,1,0:T(8,128)(2,1)}, bf16[1,192,4096]{2,1,0:T(8,128)(2,1)}, bf16[1,192,4096]{2,1,0:T(8,128)(2,1)}) custom-call(bf16[128,4096]{1,0:T(8,128)(2,1)} %tok_ref.1, bf16[128,4096]{1,0:T(8,128)(2,1)} %cot_ref.1, s32[1,128]{1,0:T(1,128)} %bitcast.9, bf16[1,128]{1,0:T(2,128)(2,1)} %bitcast.11, ...), custom_call_target="tpu_custom_call" | custom-call | tf_op jit(solution)/shard_map/pallas_call | solution.py:484
  220.4 6.5 %shard_map.111 = (bf16[128,4096]{1,0:T(8,128)(2,1)}, bf16[1,128]{1,0:T(2,128)(2,1)}, bf16[1,192,4096]{2,1,0:T(8,128)(2,1)}, bf16[1,192,4096]{2,1,0:T(8,128)(2,1)}, bf16[1,192,4096]{2,1,0:T(8,128)(2,1)}) custom-call(bf16[16,64,1152]{2,1,0:T(8,128)(2,1)} %get-tuple-element.14.back_hbm, s32[1,128]{1,0:T(1,128)} %bitcast.10, bf16[1,128]{1,0:T(2,128)(2,1)} %bitcast.12, ...), custom_call_target="tpu_custom_call" | custom-call | tf_op jit(solution)/shard_map/pallas_call | solution.py:534
